TPU v7x, 256 devices: a whole 4x4x8 slice. The times are simulated.
256 devices in a mesh: section: 8 (over z_lo, core), dp: 32 (over y, x, z_hi).
Axes of the slice: x: 4, y: 4, z: 8 (z_hi: 2, z_lo: 4; z = z_hi * 4 + z_lo), core: 2. Of those that a mesh axis runs over, the one named last changes fastest.
Arguments:
- byte_ids: int32 [2, 8192, 8], P(None, 'dp'), may hold values from 0 to 255
- patch_len: int32 [2, 8192], P(None, 'dp'), may hold values from 1 to 8
- table: bfloat16 [256, 4096], replicated, may hold values from -12 to 12
- basis: bfloat16 [4096, 256], replicated, may hold values from -0.09375 to 0.09375
- w_down: bfloat16 [8, 4096, 256], P('section'), may hold values from -0.09375 to 0.09375
- w_up: bfloat16 [8, 4096, 256], P('section'), may hold values from -0.375 to 0.375
- dcoef: bfloat16 [2, 8192, 256], P(None, 'dp'), may hold values from -0.046875 to 0.046875
Outputs:
- grad_down: bfloat16 [8, 4096, 256], P('section')
Inputs may be any that keep to these rules, and one draw needn't show every extreme that they name: `byte_ids`: slots at or past a patch's length are ignored.
All inputs are finite; a program needn't handle non-finite values.
Results may differ from a plain program's by a relative error of at most 0.035.
Values may be sent and summed in bfloat16 or wider, within the bound.
A program may use at most 128 MiB of HBM per device.

v0:
```python
import jax
import jax.numpy as jnp
from jax import lax
from jax.sharding import PartitionSpec as P


def from_behind(value, axis, steps):
    count = lax.axis_size(axis)
    first, last = (max(0, -steps), min(count, count - steps))
    return lax.ppermute(value, axis, [(source, source + steps) for source in range(first, last)])


def embed_all(byte_ids, patch_len, table):
    slots = lax.broadcasted_iota(jnp.int32, byte_ids.shape, 2)
    live = slots < patch_len[:, :, None]
    codes = lax.broadcasted_iota(jnp.int32, (1, 1, 1, table.shape[0]), 3)
    counts = jnp.sum(
        jnp.where((byte_ids[:, :, :, None] == codes) & live[:, :, :, None], 1.0, 0.0), axis=2
    )
    summed = jnp.einsum(
        "mpv,vd->mpd", counts.astype(jnp.bfloat16), table, preferred_element_type=jnp.float32
    )
    pre = summed * lax.rsqrt(patch_len.astype(jnp.float32))[:, :, None]
    return jax.nn.silu(pre).astype(jnp.bfloat16)


def forward_section(coefs, anchor, basis, weight_down, weight_up):
    xfull = anchor.astype(jnp.float32) + jnp.einsum(
        "pr,dr->pd", coefs, basis, preferred_element_type=jnp.float32
    )
    scale = lax.rsqrt(jnp.mean(xfull * xfull, axis=-1, keepdims=True) + 1e-06)
    normed = (xfull * scale).astype(jnp.bfloat16)
    zvalue = jnp.dot(normed, weight_down, preferred_element_type=jnp.float32)
    active = jax.nn.silu(zvalue).astype(jnp.bfloat16)
    branch = jnp.einsum("pk,dk->pd", active, weight_up, preferred_element_type=jnp.float32).astype(
        jnp.bfloat16
    )
    outputs = (
        coefs.astype(jnp.float32) + jnp.dot(branch, basis, preferred_element_type=jnp.float32)
    ).astype(jnp.bfloat16)
    return (outputs, (xfull, normed, zvalue))


def backward_section(upstream, xfull, zvalue, basis, weight_down, weight_up):
    scale = lax.rsqrt(jnp.mean(xfull * xfull, axis=-1, keepdims=True) + 1e-06)
    grad_branch = jnp.einsum(
        "pr,dr->pd", upstream, basis, preferred_element_type=jnp.float32
    ).astype(jnp.bfloat16)
    grad_active = jnp.dot(grad_branch, weight_up, preferred_element_type=jnp.float32)
    sigma = jax.nn.sigmoid(zvalue)
    grad_z = (grad_active * sigma * (1.0 + zvalue * (1.0 - sigma))).astype(jnp.bfloat16)
    grad_normed = jnp.einsum("pk,dk->pd", grad_z, weight_down, preferred_element_type=jnp.float32)
    hfloat = xfull * scale
    grad_x = (
        scale * (grad_normed - hfloat * jnp.mean(grad_normed * hfloat, axis=-1, keepdims=True))
    ).astype(jnp.bfloat16)
    previous = (
        upstream.astype(jnp.float32) + jnp.dot(grad_x, basis, preferred_element_type=jnp.float32)
    ).astype(jnp.bfloat16)
    return (previous, grad_z)


def place_slot(stacked, value, index, active):
    former = lax.dynamic_index_in_dim(stacked, index, 0, keepdims=False)
    return lax.dynamic_update_index_in_dim(stacked, jnp.where(active, value, former), index, 0)


def on_device(byte_ids, patch_len, table, basis, w_down, w_up, dcoef):
    sections = lax.axis_size("section")
    position = lax.axis_index("section")
    weight_down = w_down[0]
    weight_up = w_up[0]
    batches, rows_here, _ = byte_ids.shape
    width = basis.shape[0]
    ranks = basis.shape[1]
    hidden = weight_down.shape[1]
    anchors = embed_all(byte_ids, patch_len, table)
    tick_count = batches + sections - 1

    def forward_tick(moment, state):
        incoming, store_x, store_h, store_z = state
        batch_no = moment - position
        active = (batch_no >= 0) & (batch_no < batches)
        index = jnp.clip(batch_no, 0, batches - 1)
        anchor = lax.dynamic_index_in_dim(anchors, index, 0, keepdims=False)
        inputs = jnp.where(position == 0, jnp.zeros_like(incoming), incoming)
        outputs, saved = forward_section(inputs, anchor, basis, weight_down, weight_up)
        store_x = place_slot(store_x, saved[0], index, active)
        store_h = place_slot(store_h, saved[1], index, active)
        store_z = place_slot(store_z, saved[2], index, active)
        incoming = from_behind(outputs, "section", 1)
        return (incoming, store_x, store_h, store_z)

    start_state = (
        jnp.zeros((rows_here, ranks), jnp.bfloat16),
        jnp.zeros((batches, rows_here, width), jnp.float32),
        jnp.zeros((batches, rows_here, width), jnp.bfloat16),
        jnp.zeros((batches, rows_here, hidden), jnp.float32),
    )
    _, store_x, store_h, store_z = lax.fori_loop(0, tick_count, forward_tick, start_state)

    def backward_tick(moment, state):
        incoming, store_dz = state
        batch_no = moment - (sections - 1 - position)
        active = (batch_no >= 0) & (batch_no < batches)
        index = jnp.clip(batch_no, 0, batches - 1)
        last = lax.dynamic_index_in_dim(dcoef, index, 0, keepdims=False)
        upstream = jnp.where(position == sections - 1, last, incoming)
        xfull = lax.dynamic_index_in_dim(store_x, index, 0, keepdims=False)
        zvalue = lax.dynamic_index_in_dim(store_z, index, 0, keepdims=False)
        previous, grad_z = backward_section(upstream, xfull, zvalue, basis, weight_down, weight_up)
        store_dz = place_slot(store_dz, grad_z, index, active)
        incoming = from_behind(previous, "section", -1)
        return (incoming, store_dz)

    back_state = (
        jnp.zeros((rows_here, ranks), jnp.bfloat16),
        jnp.zeros((batches, rows_here, hidden), jnp.bfloat16),
    )
    _, store_dz = lax.fori_loop(0, tick_count, backward_tick, back_state)
    flat_h = store_h.reshape(batches * rows_here, width)
    flat_dz = store_dz.reshape(batches * rows_here, hidden)
    total = lax.psum(
        jnp.einsum("nd,nk->dk", flat_h, flat_dz, preferred_element_type=jnp.float32).astype(
            jnp.bfloat16
        ),
        "dp",
    )
    return total[None]


def solution(mesh):
    return jax.shard_map(
        on_device,
        mesh=mesh,
        in_specs=(
            P(None, "dp", None),
            P(None, "dp"),
            P(),
            P(),
            P("section", None, None),
            P("section", None, None),
            P(None, "dp", None),
        ),
        out_specs=P("section", None, None),
        check_vma=False,
    )
```

profile of v0, /device:TPU:2, one launch (start us, length us, event | category | flops | bytes accessed | tf_op | source)
XLA Modules:
  0.0 876.3 jit_solution(17784554316764977733)
XLA Ops:
  12.1 4.2 multiply_convert_fusion.11
  16.3 4.2 broadcast_in_dim.73
  23.1 222.9 %while.37 = (s32[]{:T(128)}, bf16[256,256]{1,0:T(8,128)(2,1)S(1)}, f32[2,256,4096]{2,1,0:T(8,128)}, bf16[2,256,4096]{2,1,0:T(8,128)(2,1)}, f32[2,256,256]{2,1,0:...) while((s32[]{:T(128)}, bf16[256,256]{1,0:T(8,128)(2,1)S(1)}, ...), condition=%wide.region_3.4_spmd, body=%wide.region_1.3_spmd.sunk | while | flops 2159739136 | bytes 71701792 | solution.py:100
  23.1 4.9 multiply_reduce_fusion.4
  47.0 4.9 multiply_reduce_fusion.4
  59.3 4.1 collective-permute-start
  73.3 4.9 multiply_reduce_fusion.4
  97.4 4.9 multiply_reduce_fusion.4
  123.5 4.9 multiply_reduce_fusion.4
  147.6 4.9 multiply_reduce_fusion.4
  173.7 4.9 multiply_reduce_fusion.4
  197.8 4.9 multiply_reduce_fusion.4
  221.9 4.9 multiply_reduce_fusion.4
  246.0 174.3 %while.38 = (s32[]{:T(128)}, bf16[256,256]{1,0:T(8,128)(2,1)S(1)}, bf16[2,256,256]{2,1,0:T(8,128)(2,1)S(1)}, pred[]{:T(512)}, s32[]{:T(128)}, /*index=5*/bf16[2,...) while((s32[]{:T(128)}, bf16[256,256]{1,0:T(8,128)(2,1)S(1)}, ...), condition=%wide.region_7.8_spmd, body=%wide.region_4.7_spmd.sunk | while | flops 2160001280 | bytes 41038632 | solution.py:120
  277.5 4.5 collective-permute-done.1
  296.8 5.0 collective-permute-done.1
  316.6 5.0 collective-permute-done.1
  336.3 5.0 collective-permute-done.1
  356.1 5.0 collective-permute-done.1
  375.8 5.0 collective-permute-done.1
  395.6 5.0 collective-permute-done.1
  415.3 5.0 collective-permute-done.1
  420.3 4.8 fusion.26
  425.2 441.2 %all-reduce.2.cloned.1.call-done = bf16[1,4096,256]{2,1,0:T(8,128)(2,1)} async-done(((bf16[1,4096,256]{2,1,0:T(8,128)(2,1)}), bf16[1,4096,256]{2,1,0:T(8,128)(2,1)}) %all-reduce.2.cloned.1.call-update) | async-done | bytes 2097168 | tf_op jit(solution)/shard_map/psum | solution.py:123
  (230 shorter events, 319.3 us)
Async XLA Ops:
  6.5 5.5 copy-start
  6.5 859.8 %all-reduce.2.cloned.1.call-start = ((), (), s32[]{:S(2)}) async-start(), calls=%async_computation | async-start | bytes 4194304 | tf_op jit(solution)/shard_map/psum | solution.py:123
  35.3 11.7 %collective-permute-start = (bf16[256,256]{1,0:T(8,128)(2,1)S(1)}, bf16[256,256]{1,0:T(8,128)(2,1)S(1)}, u32[]{:S(2)}, u32[]{:S(2)}) collective-permute-start(bf16[256,256]{1,0:T(8,128)(2,1)S(1)} %fusion.58), channel_id=1, source_target_pairs={{0,32},{32,64},{64,96},{96,128},{128,160},{160,192},{192,224},{1,3... | collective-permute-start | bytes 393224 | tf_op jit(solution)/shard_map/while/body/eval_jaxpr/ppermute | solution.py:10
  59.3 14.0 %collective-permute-start = (bf16[256,256]{1,0:T(8,128)(2,1)S(1)}, bf16[256,256]{1,0:T(8,128)(2,1)S(1)}, u32[]{:S(2)}, u32[]{:S(2)}) collective-permute-start(bf16[256,256]{1,0:T(8,128)(2,1)S(1)} %fusion.58), channel_id=1, source_target_pairs={{0,32},{32,64},{64,96},{96,128},{128,160},{160,192},{192,224},{1,3... | collective-permute-start | bytes 393224 | tf_op jit(solution)/shard_map/while/body/eval_jaxpr/ppermute | solution.py:10
  85.5 11.9 %collective-permute-start = (bf16[256,256]{1,0:T(8,128)(2,1)S(1)}, bf16[256,256]{1,0:T(8,128)(2,1)S(1)}, u32[]{:S(2)}, u32[]{:S(2)}) collective-permute-start(bf16[256,256]{1,0:T(8,128)(2,1)S(1)} %fusion.58), channel_id=1, source_target_pairs={{0,32},{32,64},{64,96},{96,128},{128,160},{160,192},{192,224},{1,3... | collective-permute-start | bytes 393224 | tf_op jit(solution)/shard_map/while/body/eval_jaxpr/ppermute | solution.py:10
  109.6 13.9 %collective-permute-start = (bf16[256,256]{1,0:T(8,128)(2,1)S(1)}, bf16[256,256]{1,0:T(8,128)(2,1)S(1)}, u32[]{:S(2)}, u32[]{:S(2)}) collective-permute-start(bf16[256,256]{1,0:T(8,128)(2,1)S(1)} %fusion.58), channel_id=1, source_target_pairs={{0,32},{32,64},{64,96},{96,128},{128,160},{160,192},{192,224},{1,3... | collective-permute-start | bytes 393224 | tf_op jit(solution)/shard_map/while/body/eval_jaxpr/ppermute | solution.py:10
  135.7 11.9 %collective-permute-start = (bf16[256,256]{1,0:T(8,128)(2,1)S(1)}, bf16[256,256]{1,0:T(8,128)(2,1)S(1)}, u32[]{:S(2)}, u32[]{:S(2)}) collective-permute-start(bf16[256,256]{1,0:T(8,128)(2,1)S(1)} %fusion.58), channel_id=1, source_target_pairs={{0,32},{32,64},{64,96},{96,128},{128,160},{160,192},{192,224},{1,3... | collective-permute-start | bytes 393224 | tf_op jit(solution)/shard_map/while/body/eval_jaxpr/ppermute | solution.py:10
  159.8 13.9 %collective-permute-start = (bf16[256,256]{1,0:T(8,128)(2,1)S(1)}, bf16[256,256]{1,0:T(8,128)(2,1)S(1)}, u32[]{:S(2)}, u32[]{:S(2)}) collective-permute-start(bf16[256,256]{1,0:T(8,128)(2,1)S(1)} %fusion.58), channel_id=1, source_target_pairs={{0,32},{32,64},{64,96},{96,128},{128,160},{160,192},{192,224},{1,3... | collective-permute-start | bytes 393224 | tf_op jit(solution)/shard_map/while/body/eval_jaxpr/ppermute | solution.py:10
  185.9 11.9 %collective-permute-start = (bf16[256,256]{1,0:T(8,128)(2,1)S(1)}, bf16[256,256]{1,0:T(8,128)(2,1)S(1)}, u32[]{:S(2)}, u32[]{:S(2)}) collective-permute-start(bf16[256,256]{1,0:T(8,128)(2,1)S(1)} %fusion.58), channel_id=1, source_target_pairs={{0,32},{32,64},{64,96},{96,128},{128,160},{160,192},{192,224},{1,3... | collective-permute-start | bytes 393224 | tf_op jit(solution)/shard_map/while/body/eval_jaxpr/ppermute | solution.py:10
  210.0 11.9 %collective-permute-start = (bf16[256,256]{1,0:T(8,128)(2,1)S(1)}, bf16[256,256]{1,0:T(8,128)(2,1)S(1)}, u32[]{:S(2)}, u32[]{:S(2)}) collective-permute-start(bf16[256,256]{1,0:T(8,128)(2,1)S(1)} %fusion.58), channel_id=1, source_target_pairs={{0,32},{32,64},{64,96},{96,128},{128,160},{160,192},{192,224},{1,3... | collective-permute-start | bytes 393224 | tf_op jit(solution)/shard_map/while/body/eval_jaxpr/ppermute | solution.py:10
  234.1 11.9 %collective-permute-start = (bf16[256,256]{1,0:T(8,128)(2,1)S(1)}, bf16[256,256]{1,0:T(8,128)(2,1)S(1)}, u32[]{:S(2)}, u32[]{:S(2)}) collective-permute-start(bf16[256,256]{1,0:T(8,128)(2,1)S(1)} %fusion.58), channel_id=1, source_target_pairs={{0,32},{32,64},{64,96},{96,128},{128,160},{160,192},{192,224},{1,3... | collective-permute-start | bytes 393224 | tf_op jit(solution)/shard_map/while/body/eval_jaxpr/ppermute | solution.py:10
  252.3 3.8 copy-start.2
  259.5 3.2 collective-permute-start.1
  276.2 5.8 collective-permute-start.1
  288.3 3.8 copy-start.2
  295.5 6.3 collective-permute-start.1
  308.1 3.8 copy-start.2
  315.3 6.3 collective-permute-start.1
  335.0 6.3 collective-permute-start.1
  354.8 6.3 collective-permute-start.1
  367.3 3.8 copy-start.2
  374.5 6.3 collective-permute-start.1
  394.3 6.3 collective-permute-start.1
  414.0 6.3 collective-permute-start.1
  (23 other events, 84.7 us)
Sparse Core Ops, SparseCore 0:
  425.3 441.0 all-reduce.1
where the time goes:
time: 880 us; the launch traced here: 876 us
  waiting for transfers between devices  483 us (55%)
  matrix products  216 us (25%)
  other arithmetic  70 us (8%)
  local copies, waits for them, and re-layouts  58.1 us (7%)
  starting transfers between devices  35 us (4%)
  between operations  13.4 us (2%)
    psum x1, waiting for transfers between devices, on_device(): lax.psum(jnp.einsum('nd,nk->dk', flat_h, flat_dz, preferred_element_type=...  441 us
    dot_general x9, matrix products, forward_section(): jnp.einsum('pr,dr->pd', coefs, basis, preferred_element_type=jnp.float32)  44.3 us
    dynamic_update_slice x18, other arithmetic, place_slot(): lax.dynamic_update_index_in_dim(stacked, jnp.where(active, value, former)...  42.1 us
    ppermute x18, waiting for transfers between devices, from_behind(): lax.ppermute(value, axis, [(source, source + steps) for source in range(f...  41.3 us
    dynamic_slice x36, local copies, waits for them, and re-layouts, place_slot(): former = lax.dynamic_index_in_dim(stacked, index, 0, keepdims=False)  40.1 us
    ppermute x18, starting transfers between devices, from_behind(): lax.ppermute(value, axis, [(source, source + steps) for source in range(f...  34.9 us
    dot_general x9, matrix products, backward_section(): jnp.einsum('pk,dk->pd', grad_z, weight_down, preferred_element_type=jnp.f...  34.2 us
    dot_general x9, matrix products, backward_section(): jnp.dot(grad_branch, weight_up, preferred_element_type=jnp.float32)  33 us
  transfers between devices with their start and end apart: 19, of which 10 were waited for; matrix products, arithmetic and copies ran while one was open for 9% of the time, Pallas kernels for 0%

commit v1 on v0

v1 whole, which is shorter than its diff:
```python
import functools

import jax
import jax.numpy as jnp
from jax import lax
from jax.experimental import pallas as pl
from jax.experimental.pallas import tpu as pltpu
from jax.sharding import PartitionSpec as P

MESH = pl.DeviceIdType.MESH
RING = 4
F32, BF16 = jnp.float32, jnp.bfloat16


def dot(a, b, dims=((1,), (0,))):
    return lax.dot_general(a, b, (dims, ((), ())), preferred_element_type=F32)


def sigmoid(v):
    return 0.5 + 0.5 * jnp.tanh(0.5 * v)


def kernel(
    ids_ref, table_hbm, basis_hbm, down_hbm, up_hbm, dcoef_ref, out_hbm,
    table, basis, down, up, emb, emb_t, part, res,
    acc_s, acc_e, counts, gram, shared, own_e, all_e,
    z_st, xb_st, r_st, c_out, d_out, c_in, d_in, small,
    big_in, mid_in, z_in, mid,
    load_sem, mu_s, mu_r, e_s, e_r, c_s, c_r, d_s, d_r, ar_s, ar_r, st_sem,
):
    sections = all_e.shape[0]
    me = lax.axis_index("section")
    dp = lax.axis_index("dp")
    zh = lax.rem(dp, 2)
    cx = lax.rem(dp // 2, RING)
    cy = dp // (2 * RING)
    width, rank = basis.shape
    rows = emb.shape[0]
    mine = rows // sections
    tiles = load_sem.shape[1]
    tile = width // tiles

    def copy_to(src, dst, ssem, rsem, where):
        return pltpu.make_async_remote_copy(
            src_ref=src, dst_ref=dst, send_sem=ssem, recv_sem=rsem,
            device_id=where, device_id_type=MESH,
        )

    def others():
        for off in range(1, sections):
            yield lax.rem(me + off, sections)

    def at(x, y, z):
        return {"dp": (y * RING + x) * 2 + z}

    def up1(v):
        return lax.rem(v + 1, RING)

    def dn1(v):
        return lax.rem(v + RING - 1, RING)

    def opp(v):
        return lax.rem(v + 2, RING)

    def load(n, i):
        src = (basis_hbm, down_hbm, up_hbm, table_hbm)[n]
        dst = (basis, down, up, table)[n]
        sl = pl.ds(pl.multiple_of(i * tile, tile), tile)
        if n == 3:
            return pltpu.make_async_copy(src.at[:, sl], dst.at[:, sl], load_sem.at[n, i])
        return pltpu.make_async_copy(src.at[sl, :], dst.at[sl, :], load_sem.at[n, i])

    for i in range(tiles):
        for n in range(3):
            load(n, i).start()
    for i in range(tiles):
        load(3, i).start()

    barrier = pltpu.get_barrier_semaphore()
    for t in others():
        pl.semaphore_signal(barrier, inc=1, device_id={"section": t}, device_id_type=MESH)
    mates = [
        at(up1(cx), cy, zh), at(dn1(cx), cy, zh), at(cx, up1(cy), zh), at(cx, dn1(cy), zh),
        at(cx, cy, 1 - zh),
    ]
    for mate in mates:
        pl.semaphore_signal(barrier, inc=1, device_id=mate, device_id_type=MESH)

    acc_s[...] = jnp.zeros_like(acc_s)

    @pl.loop(0, tiles)
    def _(i):
        for n in range(3):
            load(n, i).wait()
        sl = pl.ds(pl.multiple_of(i * tile, tile), tile)
        bt = basis[sl, :].T
        acc_s[0] += dot(bt, basis[sl, :])
        acc_s[1] += dot(bt, down[sl, :])
        acc_s[2] += dot(bt, up[sl, :])

    gram[...] = acc_s[0].astype(BF16)
    shared[pl.ds(me, 1), 0] = acc_s[1].astype(BF16)[None]
    shared[pl.ds(me, 1), 1] = acc_s[2].astype(BF16)[None]

    pl.semaphore_wait(barrier, sections - 1 + len(mates))

    def share(t):
        return copy_to(shared.at[me], shared.at[me], mu_s.at[t], mu_r.at[me], {"section": t})

    for t in others():
        share(t).start()

    codes = lax.broadcasted_iota(jnp.int32, (rows, table.shape[0]), 1)
    total = jnp.zeros(codes.shape, F32)
    for j in range(ids_ref.shape[1]):
        total += jnp.where(ids_ref[:, j : j + 1] == codes, 1.0, 0.0)
    counts[...] = total.astype(BF16)
    small[...] = lax.rsqrt(jnp.sum(total, axis=1, keepdims=True))
    acc_e[...] = jnp.zeros_like(acc_e)
    step = rows // 4

    @pl.loop(0, tiles)
    def _(i):
        load(3, i).wait()
        sl = pl.ds(pl.multiple_of(i * tile, tile), tile)
        for q in range(4):
            rs = slice(q * step, (q + 1) * step)
            pre = dot(counts[rs, :], table[:, sl]) * small[rs, :]
            anchor = (pre * sigmoid(pre)).astype(BF16)
            emb[rs, sl] = anchor
            acc_e[rs, :] += dot(anchor, down[sl, :])

    own_e[...] = acc_e[...].astype(BF16)

    def slot(t):
        return pl.ds(pl.multiple_of(t * mine, mine), mine)

    def give_e(t):
        return copy_to(own_e.at[slot(t)], all_e.at[me], e_s.at[t], e_r.at[me], {"section": t})

    for t in others():
        give_e(t).start()
    all_e[pl.ds(me, 1)] = own_e[slot(me), :][None]

    fb = jnp.zeros((mine, rank), F32)
    e2 = jnp.zeros((mine, 1), F32)
    for i in range(tiles):
        piece = emb[slot(me), i * tile : (i + 1) * tile]
        fb += dot(piece, basis[i * tile : (i + 1) * tile, :])
        wide = piece.astype(F32)
        e2 += jnp.sum(wide * wide, axis=1, keepdims=True)

    @pl.loop(0, tiles)
    def _(i):
        sl = pl.ds(pl.multiple_of(i * tile, tile), tile)
        for q in range(4):
            rs = slice(q * step, (q + 1) * step)
            emb_t[sl, rs] = emb[rs, sl].T

    def give_c(s):
        return copy_to(c_out.at[s], c_in.at[slot(me)], c_s.at[s], c_r.at[me], {"section": s})

    def give_d(s):
        return copy_to(d_out.at[s], d_in.at[slot(me)], d_s.at[s], d_r.at[me], {"section": s})

    inv = 1.0 / width
    coef = jnp.zeros((mine, rank), F32)
    for s in range(sections):

        @pl.when(me != s)
        def _():
            copy_to(own_e.at[slot(s)], all_e.at[s], e_s.at[s], e_r.at[s], {"section": s}).wait_recv()
            copy_to(shared.at[s], shared.at[s], mu_s.at[s], mu_r.at[s], {"section": s}).wait_recv()

        cb = coef.astype(BF16)
        c_out[s] = cb

        @pl.when(me != s)
        def _():
            give_c(s).start()

        zin = all_e[s].astype(F32)
        xb = fb
        sq = e2
        if s > 0:
            zin = zin + dot(cb, shared[s, 0])
            cg = dot(cb, gram[...])
            xb = xb + cg
            sq = sq + jnp.sum(coef * (fb + xb), axis=1, keepdims=True)
        r = lax.rsqrt(jnp.maximum(sq, 0.0) * inv + 1e-06)
        z = r * zin
        z_st[s] = z
        xb_st[s] = xb
        r_st[s] = r
        act = (z * sigmoid(z)).astype(BF16)
        if s < sections - 1:
            coef = coef + dot(act, shared[s, 1], ((1,), (1,)))

    grad = dcoef_ref[slot(me), :].astype(F32)
    for s in reversed(range(sections)):
        da = dot(grad.astype(BF16), shared[s, 1])
        z = z_st[s]
        r = r_st[s]
        sig = sigmoid(z)
        dz = da * sig * (1.0 + z * (1.0 - sig))
        d_out[s] = (r * dz).astype(BF16)

        @pl.when(me != s)
        def _():
            give_d(s).start()

        if s > 0:
            mean = jnp.sum(dz * z, axis=1, keepdims=True) * inv
            back = dot(dz.astype(BF16), shared[s, 0], ((1,), (1,)))
            grad = grad + r * (back - (r * mean) * xb_st[s])

    c_in[slot(me), :] = c_out[pl.ds(me, 1)][0]
    d_in[slot(me), :] = d_out[pl.ds(me, 1)][0]
    for t in others():
        copy_to(c_out.at[t], c_in.at[slot(t)], c_s.at[t], c_r.at[t], {"section": t}).wait_recv()
        copy_to(d_out.at[t], d_in.at[slot(t)], d_s.at[t], d_r.at[t], {"section": t}).wait_recv()
    for t in others():
        share(t).wait_send()
        give_e(t).wait_send()
        give_c(t).wait_send()
        give_d(t).wait_send()

    gram[...] = dot(c_in[...].T, d_in[...]).astype(BF16)
    piece_rows = width // 16

    @pl.loop(0, 16)
    def _(i):
        sl = pl.ds(pl.multiple_of(i * piece_rows, piece_rows), piece_rows)
        part[sl, :] = (dot(emb_t[sl, :], d_in[...]) + dot(basis[sl, :], gram[...])).astype(BF16)

    half, b1, b2 = width // 2, width // 8, width // 32
    first = [cx, cy]
    second = [cy, cx]

    def along(h, stage, v):
        if (h == 0) == (stage == 0):
            return at(v, cy, zh)
        return at(cx, v, zh)

    def rows_at(start, size):
        return pl.ds(pl.multiple_of(start, size), size)

    def add_into(dst, dst_rows, *others_):
        total_ = dst[dst_rows, :].astype(F32)
        for o in others_:
            total_ += o.astype(F32)
        dst[dst_rows, :] = total_.astype(BF16)

    def scatter(h, stage):
        if stage == 0:
            buf, base, size, pos, land = part, h * half, b1, first[h], big_in
        else:
            buf, base, size, pos, land = mid.at[h], 0, b2, second[h], mid_in
        hf = size // 2
        n0 = h * 21 + stage * 6
        right, left, far = up1(pos), dn1(pos), opp(pos)

        def blk(owner, part_no):
            return rows_at(base + owner * size + part_no * hf, hf)

        def cp(k, owner, part_no, to):
            return copy_to(
                buf.at[blk(owner, part_no)], land.at[h, k], ar_s.at[n0 + k], ar_r.at[n0 + k],
                along(h, stage, to),
            )

        moves = [
            cp(0, far, 0, right), cp(1, far, 1, left), cp(2, right, 1, right),
            cp(3, left, 0, left), cp(4, right, 0, right), cp(5, left, 1, left),
        ]

        def begin():
            for k in range(4):
                moves[k].start()

        def middle():
            moves[0].wait_recv()
            add_into(buf, blk(right, 0), land[h, 0])
            moves[4].start()
            moves[1].wait_recv()
            add_into(buf, blk(left, 1), land[h, 1])
            moves[5].start()

        def end(dst, dst_row):
            moves[3].wait_recv()
            moves[4].wait_recv()
            dst[dst_row : dst_row + hf, :] = (
                buf[blk(pos, 0), :].astype(F32) + land[h, 3].astype(F32) + land[h, 4].astype(F32)
            ).astype(BF16)
            moves[2].wait_recv()
            moves[5].wait_recv()
            dst[dst_row + hf : dst_row + size, :] = (
                buf[blk(pos, 1), :].astype(F32) + land[h, 2].astype(F32) + land[h, 5].astype(F32)
            ).astype(BF16)

        def finish():
            for m in moves:
                m.wait_send()

        return begin, middle, end, finish

    def gather(h, stage):
        if stage == 0:
            base, size, pos = h * half, b1, first[h]
        else:
            base, size, pos = h * half + first[h] * b1, b2, second[h]
        hf = size // 2
        n0 = h * 21 + 13 + stage * 4
        right, left = up1(pos), dn1(pos)

        def cp(k, owner, off, n, to):
            sl = rows_at(base + owner * size + off, n)
            return copy_to(
                res.at[sl], res.at[sl], ar_s.at[n0 + k], ar_r.at[n0 + k], along(h, stage, to)
            )

        moves = [
            cp(0, pos, 0, size, right), cp(1, pos, 0, size, left),
            cp(2, left, 0, hf, right), cp(3, right, hf, hf, left),
        ]

        def begin():
            moves[0].start()
            moves[1].start()

        def middle():
            moves[0].wait_recv()
            moves[2].start()
            moves[1].wait_recv()
            moves[3].start()

        def end():
            moves[2].wait_recv()
            moves[3].wait_recv()

        def finish():
            for m in moves:
                m.wait_send()

        return begin, middle, end, finish

    rs1 = [scatter(h, 0) for h in range(2)]
    rs2 = [scatter(h, 1) for h in range(2)]
    ag2 = [gather(h, 1) for h in range(2)]
    ag1 = [gather(h, 0) for h in range(2)]
    for h in range(2):
        rs1[h][0]()
    for h in range(2):
        rs1[h][1]()
    for h in range(2):
        rs1[h][2](mid.at[h], 0)
        rs2[h][0]()
    for h in range(2):
        rs2[h][1]()
    swaps = []
    for h in range(2):
        rs2[h][2](mid.at[h], 4 * b2)
        swap = copy_to(
            mid.at[h, pl.ds(4 * b2, b2)], z_in.at[h], ar_s.at[h * 21 + 12], ar_r.at[h * 21 + 12],
            at(cx, cy, 1 - zh),
        )
        swap.start()
        swaps.append(swap)
    for h in range(2):
        swaps[h].wait_recv()
        sl = rows_at(h * half + first[h] * b1 + second[h] * b2, b2)
        res[sl, :] = (mid[h, 4 * b2 :, :].astype(F32) + z_in[h].astype(F32)).astype(BF16)
        ag2[h][0]()
    for h in range(2):
        ag2[h][1]()
    for h in range(2):
        ag2[h][2]()
        ag1[h][0]()
    for h in range(2):
        ag1[h][1]()
    for h in range(2):
        ag1[h][2]()
    store = pltpu.make_async_copy(res, out_hbm, st_sem)
    store.start()
    for h in range(2):
        for g in (rs1, rs2, ag2, ag1):
            g[h][3]()
        swaps[h].wait_send()
    store.wait()


def on_device(byte_ids, patch_len, table, basis, w_down, w_up, dcoef):
    sections = lax.axis_size("section")
    batches, here, slots = byte_ids.shape
    rows = batches * here
    width, rank = basis.shape
    hidden = w_down.shape[2]
    mine = rows // sections
    tiles = 8
    live = lax.broadcasted_iota(jnp.int32, byte_ids.shape, 2) < patch_len[:, :, None]
    ids = jnp.where(live, byte_ids, -1).reshape(rows, slots)
    half, b1, b2 = width // 2, width // 8, width // 32
    vmem = pl.BlockSpec(memory_space=pltpu.VMEM)
    hbm = pl.BlockSpec(memory_space=pl.ANY)
    dma = pltpu.SemaphoreType.DMA
    scratch = [
        pltpu.VMEM((table.shape[0], width), BF16),
        pltpu.VMEM((width, rank), BF16),
        pltpu.VMEM((width, hidden), BF16),
        pltpu.VMEM((width, hidden), BF16),
        pltpu.VMEM((rows, width), BF16),
        pltpu.VMEM((width, rows), BF16),
        pltpu.VMEM((width, hidden), BF16),
        pltpu.VMEM((width, hidden), BF16),
        pltpu.VMEM((3, rank, hidden), F32),
        pltpu.VMEM((rows, hidden), F32),
        pltpu.VMEM((rows, table.shape[0]), BF16),
        pltpu.VMEM((rank, hidden), BF16),
        pltpu.VMEM((sections, 2, rank, hidden), BF16),
        pltpu.VMEM((rows, hidden), BF16),
        pltpu.VMEM((sections, mine, hidden), BF16),
        pltpu.VMEM((sections, mine, hidden), F32),
        pltpu.VMEM((sections, mine, rank), F32),
        pltpu.VMEM((sections, mine, 1), F32),
        pltpu.VMEM((sections, mine, rank), BF16),
        pltpu.VMEM((sections, mine, hidden), BF16),
        pltpu.VMEM((rows, rank), BF16),
        pltpu.VMEM((rows, hidden), BF16),
        pltpu.VMEM((rows, 1), F32),
        pltpu.VMEM((2, 6, b1 // 2, hidden), BF16),
        pltpu.VMEM((2, 6, b2 // 2, hidden), BF16),
        pltpu.VMEM((2, b2, hidden), BF16),
        pltpu.VMEM((2, b1 + b2, hidden), BF16),
        dma((4, tiles)),
        dma((sections,)), dma((sections,)), dma((sections,)), dma((sections,)),
        dma((sections,)), dma((sections,)), dma((sections,)), dma((sections,)),
        dma((42,)), dma((42,)), dma,
    ]
    out = pl.pallas_call(
        kernel,
        out_shape=jax.ShapeDtypeStruct((width, hidden), BF16),
        in_specs=[vmem, hbm, hbm, hbm, hbm, vmem],
        out_specs=hbm,
        scratch_shapes=scratch,
        compiler_params=pltpu.CompilerParams(
            collective_id=0, has_side_effects=True, vmem_limit_bytes=56 * 1024 * 1024
        ),
    )(ids, table, basis, w_down[0], w_up[0], dcoef.reshape(rows, rank))
    return out[None]


def solution(mesh):
    return jax.shard_map(
        on_device,
        mesh=mesh,
        in_specs=(
            P(None, "dp", None),
            P(None, "dp"),
            P(),
            P(),
            P("section", None, None),
            P("section", None, None),
            P(None, "dp", None),
        ),
        out_specs=P("section", None, None),
        check_vma=False,
    )
```

time: 880 us -> 131 us (0.15)
  waiting for transfers between devices: 483 us -> 0 us
  matrix products: 216 us -> 0 us
  Pallas kernels: 0 us -> 125 us
  other arithmetic: 70 us -> 0.72 us
  local copies, waits for them, and re-layouts: 58.1 us -> 3.88 us
  starting transfers between devices: 35 us -> 0 us
  between operations: 13.4 us -> 0.01 us
    psum x1 -> x0, waiting for transfers between devices: 441 us -> none  [on_device(): lax.psum(jnp.einsum('nd,nk->dk', flat_h, flat_dz, preferred_element_type=...]
    dot_general x56 -> x0, matrix products: 216 us -> none  [the longest x9 44.3 us: forward_section(): jnp.einsum('pr,dr->pd', coefs, basis, preferred_element_type=jnp.float32)]
    pallas_call x0 -> x1, Pallas kernels: none -> 125 us  [on_device(): pl.pallas_call(kernel, out_shape=jax.ShapeDtypeStruct((width, hidden), BF...]
    dynamic_update_slice x18 -> x0, other arithmetic: 42.1 us -> none  [place_slot(): lax.dynamic_update_index_in_dim(stacked, jnp.where(active, value, former)...]
    ppermute x18 -> x0, waiting for transfers between devices: 41.3 us -> none  [from_behind(): lax.ppermute(value, axis, [(source, source + steps) for source in range(f...]
    dynamic_slice x36 -> x0, local copies, waits for them, and re-layouts: 40.1 us -> none  [place_slot(): former = lax.dynamic_index_in_dim(stacked, index, 0, keepdims=False)]
    ppermute x18 -> x0, starting transfers between devices: 34.9 us -> none  [from_behind(): lax.ppermute(value, axis, [(source, source + steps) for source in range(f...]
    reduce_sum x10 -> x0, other arithmetic: 26 us -> none  [the longest x9 23 us: backward_section(): scale = lax.rsqrt(jnp.mean(xfull * xfull, axis=-1, keepdims=True) + 1e-06)]
  transfers between devices with their start and end apart: 19 -> 0, of which waited for: 10 -> 0; matrix products, arithmetic and copies ran while one was open for 9% -> 0% of each run, Pallas kernels for 0% -> 0%
where the time goes in v1:
time: 131 us; the launch traced here: 130 us
  Pallas kernels  125 us (95%)
  local copies, waits for them, and re-layouts  3.88 us (3%)
    pallas_call x1, Pallas kernels, on_device(): pl.pallas_call(kernel, out_shape=jax.ShapeDtypeStruct((width, hidden), BF...  125 us
    unnamed x1, local copies, waits for them, and re-layouts  3.05 us

profile of v1, /device:TPU:2, one launch (start us, length us, event | category | flops | bytes accessed | tf_op | source)
XLA Modules:
  0.0 129.5 jit_solution(1034159319083185242)
XLA Ops:
  0.0 0.7 fusion
  0.7 0.8 copy.8
  1.6 124.9 %shard_map.73 = bf16[4096,256]{1,0:T(8,128)(2,1)} custom-call(s32[512,8]{1,0:T(8,128)} %bitcast.8, bf16[256,4096]{1,0:T(8,128)(2,1)} %table_hbm.1, bf16[4096,256]{1,0:T(8,128)(2,1)} %basis_hbm.1, bf16[4096,256]{1,0:T(8,128)(2,1)} %bitcast.6, bf16[4096,256]{1,0:T(8,128)(2,1)} %bitcast.7, bf16[512,256]{1,0:T(8,128)(2,1)} %bitcast.9), custom_call_target="tpu_custom_call" | custom-call | tf_op jit(solution)/shard_map/pallas_call | solution.py:439
  126.5 3.0 %copy.10 = bf16[1,4096,256]{2,1,0:T(8,128)(2,1)} copy(bf16[1,4096,256]{2,1,0:T(8,128)(2,1)} %bitcast.5) | data formatting | bytes 4194304

commit v2 on v1

v2 whole, which is shorter than its diff:
```python
import functools

import jax
import jax.numpy as jnp
from jax import lax
from jax.experimental import pallas as pl
from jax.experimental.pallas import tpu as pltpu
from jax.sharding import PartitionSpec as P

MESH = pl.DeviceIdType.MESH
RING = 4
F32, BF16 = jnp.float32, jnp.bfloat16
STREAMS = 4
TIMES = {
    4: ((0, 4.2, 8.4, 13, 18.5, 23, 28, 32), (1, 2.8, 2.8, 2.8, 2.8, 2.8, 2.8, 2.8)),
    8: ((0, 3.5, 7, 11.2, 16.7, 21, 25, 28.5), (0.6, 1.4, 1.4, 1.4, 1.4, 1.4, 1.4, 1.6)),
}


def dot(a, b, dims=((1,), (0,))):
    return lax.dot_general(a, b, (dims, ((), ())), preferred_element_type=F32)


def sigmoid(v):
    return 0.5 + 0.5 * jnp.tanh(0.5 * v)


def kernel(
    streams, times,
    ids_ref, table_hbm, basis_hbm, down_hbm, up_hbm, dcoef_ref, out_hbm,
    table, basis, down, up, emb, emb_t, part, res,
    acc_s, acc_e, counts, gram, shared, own_e, all_e,
    z_st, xb_st, r_st, c_out, d_out, c_in, d_in, small, hop_out, hop_in,
    big_in, mid, mid_in, z_in,
    load_sem, mu_s, mu_r, e_s, e_r, c_s, c_r, d_s, d_r, hop_s, hop_r, ar_s, ar_r, st_sem,
):
    sections = lax.axis_size("section")
    group = all_e.shape[0]
    me = lax.axis_index("section")
    dp = lax.axis_index("dp")
    zh = lax.rem(dp, 2)
    cx = lax.rem(dp // 2, RING)
    cy = dp // (2 * RING)
    width, rank = basis.shape
    rows = emb.shape[0]
    mine = rows // group
    tiles = load_sem.shape[1]
    tile = width // tiles
    side = me // group
    here = lax.rem(me, group)
    partner = lax.rem(me + group, sections)

    def copy_to(src, dst, ssem, rsem, where):
        return pltpu.make_async_remote_copy(
            src_ref=src, dst_ref=dst, send_sem=ssem, recv_sem=rsem,
            device_id=where, device_id_type=MESH,
        )

    def others():
        for off in range(1, group):
            yield lax.rem(here + off, group)

    def device(t):
        return {"section": side * group + t}

    def at(x, y, z):
        return {"dp": (y * RING + x) * 2 + z}

    def turn(v, k):
        return lax.rem(v + k, RING)

    def load(n, i):
        src = (basis_hbm, down_hbm, up_hbm, table_hbm)[n]
        dst = (basis, down, up, table)[n]
        sl = pl.ds(pl.multiple_of(i * tile, tile), tile)
        if n == 3:
            return pltpu.make_async_copy(src.at[:, sl], dst.at[:, sl], load_sem.at[n, i])
        return pltpu.make_async_copy(src.at[sl, :], dst.at[sl, :], load_sem.at[n, i])

    for i in range(tiles):
        for n in range(3):
            load(n, i).start()
    for i in range(tiles):
        load(3, i).start()

    barrier = pltpu.get_barrier_semaphore()
    mates = [device(t) for t in others()] + [{"section": partner}]
    mates += [at(turn(cx, k), cy, zh) for k in range(1, RING)]
    mates += [at(cx, turn(cy, k), zh) for k in range(1, RING)]
    mates += [at(cx, cy, 1 - zh)]
    for mate in mates:
        pl.semaphore_signal(barrier, inc=1, device_id=mate, device_id_type=MESH)

    acc_s[...] = jnp.zeros_like(acc_s)

    @pl.loop(0, tiles)
    def _(i):
        for n in range(3):
            load(n, i).wait()
        sl = pl.ds(pl.multiple_of(i * tile, tile), tile)
        bt = basis[sl, :].T
        acc_s[0] += dot(bt, basis[sl, :])
        acc_s[1] += dot(bt, down[sl, :])
        acc_s[2] += dot(bt, up[sl, :])

    gram[...] = acc_s[0].astype(BF16)
    shared[pl.ds(here, 1), 0] = acc_s[1].astype(BF16)[None]
    shared[pl.ds(here, 1), 1] = acc_s[2].astype(BF16)[None]

    pl.semaphore_wait(barrier, len(mates))

    twin = here + 1 - 2 * lax.rem(here, 2)
    far = lax.rem(here + 2, group)
    far_twin = lax.rem(twin + 2, group)

    def share(k, what, to):
        return copy_to(shared.at[what], shared.at[what], mu_s.at[k], mu_r.at[k], device(to))

    share(1, here, far).start()
    share(0, here, twin).start()

    codes = lax.broadcasted_iota(jnp.int32, (rows, table.shape[0]), 1)
    total = jnp.zeros(codes.shape, F32)
    for j in range(ids_ref.shape[1]):
        total += jnp.where(ids_ref[:, j : j + 1] == codes, 1.0, 0.0)
    counts[...] = total.astype(BF16)
    small[...] = lax.rsqrt(jnp.sum(total, axis=1, keepdims=True))
    acc_e[...] = jnp.zeros_like(acc_e)
    step = rows // 4

    @pl.loop(0, tiles)
    def _(i):
        load(3, i).wait()
        sl = pl.ds(pl.multiple_of(i * tile, tile), tile)
        for q in range(4):
            rs = slice(q * step, (q + 1) * step)
            pre = dot(counts[rs, :], table[:, sl]) * small[rs, :]
            anchor = (pre * sigmoid(pre)).astype(BF16)
            emb[rs, sl] = anchor
            acc_e[rs, :] += dot(anchor, down[sl, :])

    own_e[...] = acc_e[...].astype(BF16)

    def slot(t):
        return pl.ds(pl.multiple_of(t * mine, mine), mine)

    def give_e(t):
        return copy_to(own_e.at[slot(t)], all_e.at[here], e_s.at[t], e_r.at[here], device(t))

    for t in others():
        give_e(t).start()
    all_e[pl.ds(here, 1)] = own_e[slot(here), :][None]

    fb = jnp.zeros((mine, rank), F32)
    e2 = jnp.zeros((mine, 1), F32)
    for i in range(tiles):
        piece = emb[slot(here), i * tile : (i + 1) * tile]
        fb += dot(piece, basis[i * tile : (i + 1) * tile, :])
        wide = piece.astype(F32)
        e2 += jnp.sum(wide * wide, axis=1, keepdims=True)

    share(1, far, far).wait_recv()
    share(2, far, twin).start()

    @pl.loop(0, tiles)
    def _(i):
        sl = pl.ds(pl.multiple_of(i * tile, tile), tile)
        for q in range(4):
            rs = slice(q * step, (q + 1) * step)
            emb_t[sl, rs] = emb[rs, sl].T

    share(0, twin, twin).wait_recv()
    share(2, far_twin, twin).wait_recv()
    for t in others():
        copy_to(own_e.at[slot(t)], all_e.at[t], e_s.at[t], e_r.at[t], device(t)).wait_recv()

    def give_c(t):
        return copy_to(c_out.at[t], c_in.at[slot(here)], c_s.at[t], c_r.at[here], device(t))

    def give_d(t):
        return copy_to(d_out.at[t], d_in.at[slot(here)], d_s.at[t], d_r.at[here], device(t))

    def hop(k):
        return copy_to(hop_out.at[k], hop_in.at[k], hop_s.at[k], hop_r.at[k], {"section": partner})

    inv = 1.0 / width

    @pl.when(side == 0)
    def _():
        hop_in[0] = jnp.zeros(hop_in.shape[1:], BF16)

    @pl.when(side == 1)
    def _():
        hop(0).wait_recv()

    coef = hop_in[0].astype(F32)
    for s in range(group):
        cb = coef.astype(BF16)
        c_out[s] = cb

        @pl.when(here != s)
        def _():
            give_c(s).start()

        cg = dot(cb, gram[...])
        xb = fb + cg
        sq = e2 + jnp.sum(coef * (fb + xb), axis=1, keepdims=True)
        r = lax.rsqrt(jnp.maximum(sq, 0.0) * inv + 1e-06)
        z = r * (all_e[s].astype(F32) + dot(cb, shared[s, 0]))
        z_st[s] = z
        xb_st[s] = xb
        r_st[s] = r
        act = (z * sigmoid(z)).astype(BF16)
        coef = coef + dot(act, shared[s, 1], ((1,), (1,)))

    @pl.when(side == 0)
    def _():
        hop_out[0] = coef.astype(BF16)
        hop(0).start()
        hop(1).wait_recv()

    @pl.when(side == 1)
    def _():
        hop_in[1] = dcoef_ref[slot(here), :]

    grad = hop_in[1].astype(F32)
    for s in reversed(range(group)):
        da = dot(grad.astype(BF16), shared[s, 1])
        z = z_st[s]
        r = r_st[s]
        sig = sigmoid(z)
        dz = da * sig * (1.0 + z * (1.0 - sig))
        d_out[s] = (r * dz).astype(BF16)

        @pl.when(here != s)
        def _():
            give_d(s).start()

        mean = jnp.sum(dz * z, axis=1, keepdims=True) * inv
        back = dot(dz.astype(BF16), shared[s, 0], ((1,), (1,)))
        grad = grad + r * (back - (r * mean) * xb_st[s])

    @pl.when(side == 1)
    def _():
        hop_out[1] = grad.astype(BF16)
        hop(1).start()

    c_in[slot(here), :] = c_out[pl.ds(here, 1)][0]
    d_in[slot(here), :] = d_out[pl.ds(here, 1)][0]
    for t in others():
        copy_to(c_out.at[t], c_in.at[slot(t)], c_s.at[t], c_r.at[t], device(t)).wait_recv()
        copy_to(d_out.at[t], d_in.at[slot(t)], d_s.at[t], d_r.at[t], device(t)).wait_recv()

    gram[...] = dot(c_in[...].T, d_in[...]).astype(BF16)
    own = width // streams
    b1, b2 = own // RING, own // RING // RING
    hf = b1 // 2
    per = 17

    def rows_at(start, size):
        return pl.ds(pl.multiple_of(start, size), size)

    def along(st, stage, v):
        if st % 2 == stage:
            return at(v, cy, zh)
        return at(cx, v, zh)

    def add(*parts):
        total_ = parts[0].astype(F32)
        for p in parts[1:]:
            total_ += p.astype(F32)
        return total_.astype(BF16)

    def stream(st):
        base = st * own
        pos, pos2 = (cx, cy) if st % 2 == 0 else (cy, cx)
        right, left, opposite = turn(pos, 1), turn(pos, 3), turn(pos, 2)
        n0 = st * per

        def send(k, src, dst, to):
            return copy_to(src, dst, ar_s.at[n0 + k], ar_r.at[n0 + k], to)

        def blk(owner, part_no):
            return rows_at(base + owner * b1 + part_no * hf, hf)

        def over(k, owner, part_no, to):
            return send(k, part.at[blk(owner, part_no)], big_in.at[st, k], along(st, 0, to))

        scat = [
            over(0, opposite, 0, right), over(1, opposite, 1, left), over(2, right, 1, right),
            over(3, left, 0, left), over(4, right, 0, right), over(5, left, 1, left),
        ]

        def sub(v):
            return rows_at(v * b2, b2)

        scat2 = [
            send(5 + o, mid.at[st, sub(turn(pos2, o))], mid_in.at[st, o - 1],
                 along(st, 1, turn(pos2, o)))
            for o in range(1, RING)
        ]
        swap = send(9, mid.at[st, pl.ds(b1, b2)], z_in.at[st], at(cx, cy, 1 - zh))
        mine_sl = rows_at(base + pos * b1 + pos2 * b2, b2)
        gath2 = [
            send(9 + o, res.at[mine_sl], res.at[mine_sl], along(st, 1, turn(pos2, o)))
            for o in range(1, RING)
        ]

        def whole(k, owner, off, n, to):
            sl = rows_at(base + owner * b1 + off, n)
            return send(13 + k, res.at[sl], res.at[sl], along(st, 0, to))

        gath = [
            whole(0, pos, 0, b1, right), whole(1, pos, 0, b1, left),
            whole(2, left, 0, hf, right), whole(3, right, hf, hf, left),
        ]
        store = pltpu.make_async_copy(
            res.at[pl.ds(base, own)], out_hbm.at[pl.ds(base, own)], st_sem.at[st]
        )

        def product():
            sl = pl.ds(base, own)
            part[sl, :] = (dot(emb_t[sl, :], d_in[...]) + dot(basis[sl, :], gram[...])).astype(BF16)
            for k in range(4):
                scat[k].start()

        def pass_on():
            scat[0].wait_recv()
            part[blk(right, 0), :] = add(part[blk(right, 0), :], big_in[st, 0])
            scat[4].start()
            scat[1].wait_recv()
            part[blk(left, 1), :] = add(part[blk(left, 1), :], big_in[st, 1])
            scat[5].start()

        def block_done():
            scat[3].wait_recv()
            scat[4].wait_recv()
            mid[st, 0:hf, :] = add(part[blk(pos, 0), :], big_in[st, 3], big_in[st, 4])
            scat[2].wait_recv()
            scat[5].wait_recv()
            mid[st, hf:b1, :] = add(part[blk(pos, 1), :], big_in[st, 2], big_in[st, 5])
            for m in scat2:
                m.start()

        def sub_done():
            for m in scat2:
                m.wait_recv()
            mid[st, b1 : b1 + b2, :] = add(
                mid[st, sub(pos2), :], mid_in[st, 0], mid_in[st, 1], mid_in[st, 2]
            )
            swap.start()

        def total_done():
            swap.wait_recv()
            res[mine_sl, :] = add(mid[st, b1 : b1 + b2, :], z_in[st])
            for m in gath2:
                m.start()

        def block_back():
            for m in gath2:
                m.wait_recv()
            gath[0].start()
            gath[1].start()

        def forward():
            gath[0].wait_recv()
            gath[2].start()
            gath[1].wait_recv()
            gath[3].start()

        def out():
            gath[2].wait_recv()
            gath[3].wait_recv()
            store.start()

        def finish():
            for m in scat + scat2 + [swap] + gath2 + gath:
                m.wait_send()
            store.wait()

        return [product, pass_on, block_done, sub_done, total_done, block_back, forward, out], finish

    made = [stream(st) for st in range(streams)]
    order = sorted(
        (times[0][k] + times[1][k] * (st // 2), st, k) for st in range(streams) for k in range(8)
    )
    for _, st, k in order:
        made[st][0][k]()
    for st in range(streams):
        made[st][1]()

    share(1, here, far).wait_send()
    share(0, here, twin).wait_send()
    share(2, far, twin).wait_send()
    for t in others():
        give_e(t).wait_send()
        give_c(t).wait_send()
        give_d(t).wait_send()

    @pl.when(side == 0)
    def _():
        hop(0).wait_send()

    @pl.when(side == 1)
    def _():
        hop(1).wait_send()


def on_device(byte_ids, patch_len, table, basis, w_down, w_up, dcoef):
    sections = lax.axis_size("section")
    batches, here, slots = byte_ids.shape
    rows = batches * here
    width, rank = basis.shape
    hidden = w_down.shape[2]
    group = sections // 2
    mine = rows // group
    tiles = 8
    streams = STREAMS
    live = lax.broadcasted_iota(jnp.int32, byte_ids.shape, 2) < patch_len[:, :, None]
    ids = jnp.where(live, byte_ids, -1).reshape(rows, slots)
    b1 = width // streams // RING
    b2 = b1 // RING
    vmem = pl.BlockSpec(memory_space=pltpu.VMEM)
    hbm = pl.BlockSpec(memory_space=pl.ANY)
    dma = pltpu.SemaphoreType.DMA
    scratch = [
        pltpu.VMEM((table.shape[0], width), BF16),
        pltpu.VMEM((width, rank), BF16),
        pltpu.VMEM((width, hidden), BF16),
        pltpu.VMEM((width, hidden), BF16),
        pltpu.VMEM((rows, width), BF16),
        pltpu.VMEM((width, rows), BF16),
        pltpu.VMEM((width, hidden), BF16),
        pltpu.VMEM((width, hidden), BF16),
        pltpu.VMEM((3, rank, hidden), F32),
        pltpu.VMEM((rows, hidden), F32),
        pltpu.VMEM((rows, table.shape[0]), BF16),
        pltpu.VMEM((rank, hidden), BF16),
        pltpu.VMEM((group, 2, rank, hidden), BF16),
        pltpu.VMEM((rows, hidden), BF16),
        pltpu.VMEM((group, mine, hidden), BF16),
        pltpu.VMEM((group, mine, hidden), F32),
        pltpu.VMEM((group, mine, rank), F32),
        pltpu.VMEM((group, mine, 1), F32),
        pltpu.VMEM((group, mine, rank), BF16),
        pltpu.VMEM((group, mine, hidden), BF16),
        pltpu.VMEM((rows, rank), BF16),
        pltpu.VMEM((rows, hidden), BF16),
        pltpu.VMEM((rows, 1), F32),
        pltpu.VMEM((2, mine, rank), BF16),
        pltpu.VMEM((2, mine, rank), BF16),
        pltpu.VMEM((streams, 6, b1 // 2, hidden), BF16),
        pltpu.VMEM((streams, b1 + b2, hidden), BF16),
        pltpu.VMEM((streams, 3, b2, hidden), BF16),
        pltpu.VMEM((streams, b2, hidden), BF16),
        dma((4, tiles)), dma((3,)), dma((3,)),
        dma((group,)), dma((group,)), dma((group,)), dma((group,)), dma((group,)), dma((group,)),
        dma((2,)), dma((2,)), dma((streams * 17,)), dma((streams * 17,)), dma((streams,)),
    ]
    out = pl.pallas_call(
        functools.partial(kernel, streams, TIMES[streams]),
        out_shape=jax.ShapeDtypeStruct((width, hidden), BF16),
        in_specs=[vmem, hbm, hbm, hbm, hbm, vmem],
        out_specs=hbm,
        scratch_shapes=scratch,
        compiler_params=pltpu.CompilerParams(
            collective_id=0, has_side_effects=True, vmem_limit_bytes=56 * 1024 * 1024
        ),
    )(ids, table, basis, w_down[0], w_up[0], dcoef.reshape(rows, rank))
    return out[None]


def solution(mesh):
    return jax.shard_map(
        on_device,
        mesh=mesh,
        in_specs=(
            P(None, "dp", None),
            P(None, "dp"),
            P(),
            P(),
            P("section", None, None),
            P("section", None, None),
            P(None, "dp", None),
        ),
        out_specs=P("section", None, None),
        check_vma=False,
    )
```

time: 131 us -> 84.5 us (0.65)
  Pallas kernels: 125 us -> 78.9 us
    pallas_call x1, Pallas kernels: 125 us -> 78.9 us  [on_device(): pl.pallas_call(functools.partial(kernel, streams, TIMES[streams]), out_sh...]
where the time goes in v2:
time: 84.5 us; the launch traced here: 83.5 us
  Pallas kernels  78.9 us (93%)
  local copies, waits for them, and re-layouts  3.88 us (5%)
    pallas_call x1, Pallas kernels, on_device(): pl.pallas_call(functools.partial(kernel, streams, TIMES[streams]), out_sh...  78.9 us
    unnamed x1, local copies, waits for them, and re-layouts  3.05 us

profile of v2, /device:TPU:2, one launch (start us, length us, event | category | flops | bytes accessed | tf_op | source)
XLA Modules:
  0.0 83.5 jit_solution(4308330173940310127)
XLA Ops:
  0.0 0.7 fusion
  0.7 0.8 %copy.8 = s32[2,256,8]{2,1,0:T(8,128)} copy(s32[2,256,8]{1,2,0:T(8,128)S(1)} %fusion) | data formatting | bytes 32768 | tf_op jit(solution)/shard_map/jit(_where)/select_n | solution.py:420
  1.6 78.9 %shard_map.73 = bf16[4096,256]{1,0:T(8,128)(2,1)} custom-call(s32[512,8]{1,0:T(8,128)} %bitcast.8, bf16[256,4096]{1,0:T(8,128)(2,1)} %table_hbm.1, bf16[4096,256]{1,0:T(8,128)(2,1)} %basis_hbm.1, bf16[4096,256]{1,0:T(8,128)(2,1)} %bitcast.6, bf16[4096,256]{1,0:T(8,128)(2,1)} %bitcast.7, bf16[512,256]{1,0:T(8,128)(2,1)} %bitcast.9), custom_call_target="tpu_custom_call" | custom-call | tf_op jit(solution)/shard_map/pallas_call | solution.py:460
  80.4 3.0 %copy.10 = bf16[1,4096,256]{2,1,0:T(8,128)(2,1)} copy(bf16[1,4096,256]{2,1,0:T(8,128)(2,1)} %bitcast.5) | data formatting | bytes 4194304

commit v3 on v2

--- a/solution.py
+++ b/solution.py
@@ -12,8 +12,7 @@
 F32, BF16 = jnp.float32, jnp.bfloat16
 STREAMS = 4
 TIMES = {
-    4: ((0, 4.2, 8.4, 13, 18.5, 23, 28, 32), (1, 2.8, 2.8, 2.8, 2.8, 2.8, 2.8, 2.8)),
-    8: ((0, 3.5, 7, 11.2, 16.7, 21, 25, 28.5), (0.6, 1.4, 1.4, 1.4, 1.4, 1.4, 1.4, 1.6)),
+    4: ((0, 4.2, 4.2, 8.4, 13, 18.5, 23, 28, 28, 32), (1, 2.8, 2.8, 2.8, 2.8, 2.8, 2.8, 2.8, 2.8, 2.8)),
 }
 
 
@@ -27,7 +26,7 @@
 
 def kernel(
     streams, times,
-    ids_ref, table_hbm, basis_hbm, down_hbm, up_hbm, dcoef_ref, out_hbm,
+    ids_ref, len_ref, table_hbm, basis_hbm, down_hbm, up_hbm, dcoef_hbm, out_hbm,
     table, basis, down, up, emb, emb_t, part, res,
     acc_s, acc_e, counts, gram, shared, own_e, all_e,
     z_st, xb_st, r_st, c_out, d_out, c_in, d_in, small, hop_out, hop_in,
@@ -119,12 +118,17 @@
     share(1, here, far).start()
     share(0, here, twin).start()
 
-    codes = lax.broadcasted_iota(jnp.int32, (rows, table.shape[0]), 1)
-    total = jnp.zeros(codes.shape, F32)
-    for j in range(ids_ref.shape[1]):
-        total += jnp.where(ids_ref[:, j : j + 1] == codes, 1.0, 0.0)
-    counts[...] = total.astype(BF16)
-    small[...] = lax.rsqrt(jnp.sum(total, axis=1, keepdims=True))
+    batches, slots, here_rows = ids_ref.shape
+    codes = lax.broadcasted_iota(jnp.int32, (table.shape[0], here_rows), 0)
+    for m in range(batches):
+        total = jnp.zeros(codes.shape, F32)
+        for j in range(slots):
+            live = jnp.where(len_ref[m : m + 1, :] > j, ids_ref[m, j : j + 1, :], -1)
+            total += jnp.where(live == codes, 1.0, 0.0)
+        total = total.T
+        rs = slice(m * here_rows, (m + 1) * here_rows)
+        counts[rs, :] = total.astype(BF16)
+        small[rs, :] = lax.rsqrt(jnp.sum(total, axis=1, keepdims=True))
     acc_e[...] = jnp.zeros_like(acc_e)
     step = rows // 4
 
@@ -132,8 +136,8 @@
     def _(i):
         load(3, i).wait()
         sl = pl.ds(pl.multiple_of(i * tile, tile), tile)
-        for q in range(4):
-            rs = slice(q * step, (q + 1) * step)
+        for q in range(2):
+            rs = slice(q * rows // 2, (q + 1) * rows // 2)
             pre = dot(counts[rs, :], table[:, sl]) * small[rs, :]
             anchor = (pre * sigmoid(pre)).astype(BF16)
             emb[rs, sl] = anchor
@@ -162,12 +166,13 @@
     share(1, far, far).wait_recv()
     share(2, far, twin).start()
 
-    @pl.loop(0, tiles)
-    def _(i):
-        sl = pl.ds(pl.multiple_of(i * tile, tile), tile)
-        for q in range(4):
-            rs = slice(q * step, (q + 1) * step)
-            emb_t[sl, rs] = emb[rs, sl].T
+    def flip():
+        @pl.loop(0, tiles)
+        def _(i):
+            sl = pl.ds(pl.multiple_of(i * tile, tile), tile)
+            for q in range(4):
+                rs = slice(q * step, (q + 1) * step)
+                emb_t[sl, rs] = emb[rs, sl].T
 
     share(0, twin, twin).wait_recv()
     share(2, far_twin, twin).wait_recv()
@@ -191,17 +196,13 @@
 
     @pl.when(side == 1)
     def _():
+        flip()
         hop(0).wait_recv()
 
     coef = hop_in[0].astype(F32)
     for s in range(group):
         cb = coef.astype(BF16)
         c_out[s] = cb
-
-        @pl.when(here != s)
-        def _():
-            give_c(s).start()
-
         cg = dot(cb, gram[...])
         xb = fb + cg
         sq = e2 + jnp.sum(coef * (fb + xb), axis=1, keepdims=True)
@@ -217,11 +218,20 @@
     def _():
         hop_out[0] = coef.astype(BF16)
         hop(0).start()
+
+    for t in others():
+        give_c(t).start()
+
+    @pl.when(side == 0)
+    def _():
+        flip()
         hop(1).wait_recv()
 
     @pl.when(side == 1)
     def _():
-        hop_in[1] = dcoef_ref[slot(here), :]
+        last = pltpu.make_async_copy(dcoef_hbm.at[slot(here)], hop_in.at[1], st_sem.at[0])
+        last.start()
+        last.wait()
 
     grad = hop_in[1].astype(F32)
     for s in reversed(range(group)):
@@ -232,7 +242,7 @@
         dz = da * sig * (1.0 + z * (1.0 - sig))
         d_out[s] = (r * dz).astype(BF16)
 
-        @pl.when(here != s)
+        @pl.when((here != s) & (side == 0))
         def _():
             give_d(s).start()
 
@@ -244,6 +254,8 @@
     def _():
         hop_out[1] = grad.astype(BF16)
         hop(1).start()
+        for t in others():
+            give_d(t).start()
 
     c_in[slot(here), :] = c_out[pl.ds(here, 1)][0]
     d_in[slot(here), :] = d_out[pl.ds(here, 1)][0]
@@ -324,10 +336,12 @@
             for k in range(4):
                 scat[k].start()
 
-        def pass_on():
+        def pass_right():
             scat[0].wait_recv()
             part[blk(right, 0), :] = add(part[blk(right, 0), :], big_in[st, 0])
             scat[4].start()
+
+        def pass_left():
             scat[1].wait_recv()
             part[blk(left, 1), :] = add(part[blk(left, 1), :], big_in[st, 1])
             scat[5].start()
@@ -362,9 +376,11 @@
             gath[0].start()
             gath[1].start()
 
-        def forward():
+        def forward_right():
             gath[0].wait_recv()
             gath[2].start()
+
+        def forward_left():
             gath[1].wait_recv()
             gath[3].start()
 
@@ -378,11 +394,15 @@
                 m.wait_send()
             store.wait()
 
-        return [product, pass_on, block_done, sub_done, total_done, block_back, forward, out], finish
+        stages = [
+            product, pass_right, pass_left, block_done, sub_done, total_done, block_back,
+            forward_right, forward_left, out,
+        ]
+        return stages, finish
 
     made = [stream(st) for st in range(streams)]
     order = sorted(
-        (times[0][k] + times[1][k] * (st // 2), st, k) for st in range(streams) for k in range(8)
+        (times[0][k] + times[1][k] * (st // 2), st, k) for st in range(streams) for k in range(10)
     )
     for _, st, k in order:
         made[st][0][k]()
@@ -406,9 +426,24 @@
         hop(1).wait_send()
 
 
+def place(src, dst, hold, sem):
+    parts = sem.shape[1]
+    n = src.shape[0] // parts
+    cut = [pl.ds(i * n, n) for i in range(parts)]
+    ins = [pltpu.make_async_copy(src.at[c], hold.at[c], sem.at[0, i]) for i, c in enumerate(cut)]
+    outs = [pltpu.make_async_copy(hold.at[c], dst.at[c], sem.at[1, i]) for i, c in enumerate(cut)]
+    for m in ins:
+        m.start()
+    for m, o in zip(ins, outs):
+        m.wait()
+        o.start()
+    for o in outs:
+        o.wait()
+
+
 def on_device(byte_ids, patch_len, table, basis, w_down, w_up, dcoef):
     sections = lax.axis_size("section")
-    batches, here, slots = byte_ids.shape
+    batches, here, _ = byte_ids.shape
     rows = batches * here
     width, rank = basis.shape
     hidden = w_down.shape[2]
@@ -416,8 +451,7 @@
     mine = rows // group
     tiles = 8
     streams = STREAMS
-    live = lax.broadcasted_iota(jnp.int32, byte_ids.shape, 2) < patch_len[:, :, None]
-    ids = jnp.where(live, byte_ids, -1).reshape(rows, slots)
+    ids = jnp.transpose(byte_ids, (0, 2, 1))
     b1 = width // streams // RING
     b2 = b1 // RING
     vmem = pl.BlockSpec(memory_space=pltpu.VMEM)
@@ -460,13 +494,20 @@
     out = pl.pallas_call(
         functools.partial(kernel, streams, TIMES[streams]),
         out_shape=jax.ShapeDtypeStruct((width, hidden), BF16),
-        in_specs=[vmem, hbm, hbm, hbm, hbm, vmem],
+        in_specs=[vmem, vmem, hbm, hbm, hbm, hbm, hbm],
         out_specs=hbm,
         scratch_shapes=scratch,
         compiler_params=pltpu.CompilerParams(
             collective_id=0, has_side_effects=True, vmem_limit_bytes=56 * 1024 * 1024
         ),
-    )(ids, table, basis, w_down[0], w_up[0], dcoef.reshape(rows, rank))
+    )(ids, patch_len, table, basis, w_down[0], w_up[0], dcoef.reshape(rows, rank))
+    out = pl.pallas_call(
+        place,
+        out_shape=jax.ShapeDtypeStruct((width, hidden), BF16),
+        in_specs=[hbm],
+        out_specs=hbm,
+        scratch_shapes=[pltpu.VMEM((width, hidden), BF16), dma((2, 4))],
+    )(out)
     return out[None]
 
 

time: 84.5 us -> 82.6 us (0.978)
  local copies, waits for them, and re-layouts: 3.88 us -> 0 us
  Pallas kernels: 78.9 us -> 81.4 us
    unnamed x1 -> x0, local copies, waits for them, and re-layouts: 3.05 us -> none
    pallas_call x0 -> x1, Pallas kernels: none -> 2.42 us  [on_device(): pl.pallas_call(place, out_shape=jax.ShapeDtypeStruct((width, hidden), BF1...]
where the time goes in v3:
time: 82.6 us; the launch traced here: 81.5 us
  Pallas kernels  81.4 us (99%)
    pallas_call x1, Pallas kernels, on_device(): pl.pallas_call(functools.partial(kernel, streams, TIMES[streams]), out_sh...  79 us
    pallas_call x1, Pallas kernels, on_device(): pl.pallas_call(place, out_shape=jax.ShapeDtypeStruct((width, hidden), BF1...  2.42 us

profile of v3, /device:TPU:2, one launch (start us, length us, event | category | flops | bytes accessed | tf_op | source)
XLA Modules:
  0.0 81.5 jit_solution(5597246019391827860)
XLA Ops:
  0.0 79.0 %shard_map.73.src = bf16[4096,256]{1,0:T(8,128)(2,1)} custom-call(s32[2,8,256]{2,1,0:T(8,128)} %bitcast.8, s32[2,256]{1,0:T(2,128)} %len_ref.1, bf16[256,4096]{1,0:T(8,128)(2,1)} %table_hbm.1, bf16[4096,256]{1,0:T(8,128)(2,1)} %basis_hbm.1, bf16[4096,256]{1,0:T(8,128)(2,1)} %bitcast.5, bf16[4096,256]{1,0:T(8,128)(2,1)} %bitcast.6, bf16[512,256]{1,0:T(8,128)(2,1)} %bitcast.7), custom_call_target="tpu_custom_call" | custom-call | tf_op jit(solution)/shard_map/pallas_call | solution.py:494
  79.0 2.4 %shard_map.74 = bf16[4096,256]{1,0:T(8,128)(2,1)} custom-call(bf16[4096,256]{1,0:T(8,128)(2,1)} %shard_map.73.src), custom_call_target="tpu_custom_call" | custom-call | tf_op jit(solution)/shard_map/pallas_call | solution.py:504

commit v4 on v3

--- a/solution.py
+++ b/solution.py
@@ -11,6 +11,8 @@
 RING = 4
 F32, BF16 = jnp.float32, jnp.bfloat16
 STREAMS = 4
+HALVES = 1
+PR = 256
 TIMES = {
     4: ((0, 4.2, 4.2, 8.4, 13, 18.5, 23, 28, 28, 32), (1, 2.8, 2.8, 2.8, 2.8, 2.8, 2.8, 2.8, 2.8, 2.8)),
 }
@@ -28,8 +30,8 @@
     streams, times,
     ids_ref, len_ref, table_hbm, basis_hbm, down_hbm, up_hbm, dcoef_hbm, out_hbm,
     table, basis, down, up, emb, emb_t, part, res,
-    acc_s, acc_e, counts, gram, shared, own_e, all_e,
-    z_st, xb_st, r_st, c_out, d_out, c_in, d_in, small, hop_out, hop_in,
+    acc_s, acc_e, counts, gram, shared, turned, own_e, all_e,
+    z_st, xb_st, r_st, c_out, d_out, c_in, d_in, small, fb_st, e2_st, hop_out, hop_in,
     big_in, mid, mid_in, z_in,
     load_sem, mu_s, mu_r, e_s, e_r, c_s, c_r, d_s, d_r, hop_s, hop_r, ar_s, ar_r, st_sem,
 ):
@@ -104,7 +106,7 @@
 
     gram[...] = acc_s[0].astype(BF16)
     shared[pl.ds(here, 1), 0] = acc_s[1].astype(BF16)[None]
-    shared[pl.ds(here, 1), 1] = acc_s[2].astype(BF16)[None]
+    shared[pl.ds(here, 1), 1] = acc_s[2].T.astype(BF16)[None]
 
     pl.semaphore_wait(barrier, len(mates))
 
@@ -162,11 +164,18 @@
         fb += dot(piece, basis[i * tile : (i + 1) * tile, :])
         wide = piece.astype(F32)
         e2 += jnp.sum(wide * wide, axis=1, keepdims=True)
+    fb_st[...] = fb
+    e2_st[...] = e2
 
     share(1, far, far).wait_recv()
     share(2, far, twin).start()
 
     def flip():
+        @pl.loop(0, group)
+        def _(s):
+            for n in range(2):
+                turned[s, n] = shared[s, n].T
+
         @pl.loop(0, tiles)
         def _(i):
             sl = pl.ds(pl.multiple_of(i * tile, tile), tile)
@@ -179,89 +188,132 @@
     for t in others():
         copy_to(own_e.at[slot(t)], all_e.at[t], e_s.at[t], e_r.at[t], device(t)).wait_recv()
 
-    def give_c(t):
-        return copy_to(c_out.at[t], c_in.at[slot(here)], c_s.at[t], c_r.at[here], device(t))
-
-    def give_d(t):
-        return copy_to(d_out.at[t], d_in.at[slot(here)], d_s.at[t], d_r.at[here], device(t))
-
-    def hop(k):
-        return copy_to(hop_out.at[k], hop_in.at[k], hop_s.at[k], hop_r.at[k], {"section": partner})
+    part_rows = mine // HALVES
+
+    def cut(k):
+        return pl.ds(k * part_rows, part_rows)
+
+    def sub_slot(t, k):
+        return pl.ds(pl.multiple_of(t * mine + k * part_rows, part_rows), part_rows)
+
+    def give(out, into, ssem, rsem, t, k, source):
+        return copy_to(
+            out.at[t, cut(k)], into.at[sub_slot(source, k)], ssem.at[t, k], rsem.at[source, k],
+            device(t),
+        )
+
+    def give_c(t, k):
+        return give(c_out, c_in, c_s, c_r, t, k, here)
+
+    def give_d(t, k):
+        return give(d_out, d_in, d_s, d_r, t, k, here)
+
+    def hop(n, k):
+        return copy_to(
+            hop_out.at[n, cut(k)], hop_in.at[n, cut(k)], hop_s.at[n, k], hop_r.at[n, k],
+            {"section": partner},
+        )
 
     inv = 1.0 / width
+
+    def up_part(k, coef):
+        fb, e2 = fb_st[cut(k), :], e2_st[cut(k), :]
+
+        def step_up(s, coef):
+            cb = coef.astype(BF16)
+            c_out[s, cut(k)] = cb
+            cg = dot(cb, gram[...])
+            xb = fb + cg
+            sq = e2 + jnp.sum(coef * (fb + xb), axis=1, keepdims=True)
+            r = lax.rsqrt(jnp.maximum(sq, 0.0) * inv + 1e-06)
+            z = r * (all_e[s, cut(k)].astype(F32) + dot(cb, shared[s, 0]))
+            z_st[s, cut(k)] = z
+            xb_st[s, cut(k)] = xb
+            r_st[s, cut(k)] = r
+            act = (z * sigmoid(z)).astype(BF16)
+            return coef + dot(act, shared[s, 1])
+
+        return lax.fori_loop(0, group, step_up, coef, unroll=True)
+
+    def down_part(k, grad, then):
+        def step_down(i, grad):
+            s = group - 1 - i
+            da = dot(grad.astype(BF16), turned[s, 1])
+            z = z_st[s, cut(k)]
+            r = r_st[s, cut(k)]
+            sig = sigmoid(z)
+            dz = da * sig * (1.0 + z * (1.0 - sig))
+            d_out[s, cut(k)] = (r * dz).astype(BF16)
+            then(s)
+            mean = jnp.sum(dz * z, axis=1, keepdims=True) * inv
+            back = dot(dz.astype(BF16), turned[s, 0])
+            return grad + r * (back - (r * mean) * xb_st[s, cut(k)])
+
+        return lax.fori_loop(0, group, step_down, grad, unroll=True)
 
     @pl.when(side == 0)
     def _():
-        hop_in[0] = jnp.zeros(hop_in.shape[1:], BF16)
-
-    @pl.when(side == 1)
-    def _():
+        for k in range(HALVES):
+            coef = up_part(k, jnp.zeros((part_rows, rank), F32))
+            hop_out[0, cut(k)] = coef.astype(BF16)
+            hop(0, k).start()
+        for t in others():
+            for k in range(HALVES):
+                give_c(t, k).start()
         flip()
-        hop(0).wait_recv()
-
-    coef = hop_in[0].astype(F32)
-    for s in range(group):
-        cb = coef.astype(BF16)
-        c_out[s] = cb
-        cg = dot(cb, gram[...])
-        xb = fb + cg
-        sq = e2 + jnp.sum(coef * (fb + xb), axis=1, keepdims=True)
-        r = lax.rsqrt(jnp.maximum(sq, 0.0) * inv + 1e-06)
-        z = r * (all_e[s].astype(F32) + dot(cb, shared[s, 0]))
-        z_st[s] = z
-        xb_st[s] = xb
-        r_st[s] = r
-        act = (z * sigmoid(z)).astype(BF16)
-        coef = coef + dot(act, shared[s, 1], ((1,), (1,)))
-
-    @pl.when(side == 0)
-    def _():
-        hop_out[0] = coef.astype(BF16)
-        hop(0).start()
-
-    for t in others():
-        give_c(t).start()
-
-    @pl.when(side == 0)
-    def _():
-        flip()
-        hop(1).wait_recv()
+        for k in range(HALVES):
+            hop(1, k).wait_recv()
+
+            def send_on(s):
+                @pl.when(here != s)
+                def _():
+                    give_d(s, k).start()
+
+            down_part(k, hop_in[1, cut(k)].astype(F32), send_on)
 
     @pl.when(side == 1)
     def _():
         last = pltpu.make_async_copy(dcoef_hbm.at[slot(here)], hop_in.at[1], st_sem.at[0])
         last.start()
+        flip()
         last.wait()
-
-    grad = hop_in[1].astype(F32)
-    for s in reversed(range(group)):
-        da = dot(grad.astype(BF16), shared[s, 1])
-        z = z_st[s]
-        r = r_st[s]
-        sig = sigmoid(z)
-        dz = da * sig * (1.0 + z * (1.0 - sig))
-        d_out[s] = (r * dz).astype(BF16)
-
-        @pl.when((here != s) & (side == 0))
-        def _():
-            give_d(s).start()
-
-        mean = jnp.sum(dz * z, axis=1, keepdims=True) * inv
-        back = dot(dz.astype(BF16), shared[s, 0], ((1,), (1,)))
-        grad = grad + r * (back - (r * mean) * xb_st[s])
-
-    @pl.when(side == 1)
-    def _():
-        hop_out[1] = grad.astype(BF16)
-        hop(1).start()
+        for k in range(HALVES):
+            hop(0, k).wait_recv()
+            up_part(k, hop_in[0, cut(k)].astype(F32))
+            grad = down_part(k, hop_in[1, cut(k)].astype(F32), lambda s: None)
+            hop_out[1, cut(k)] = grad.astype(BF16)
+            hop(1, k).start()
         for t in others():
-            give_d(t).start()
+            for k in range(HALVES):
+                give_c(t, k).start()
+                give_d(t, k).start()
 
     c_in[slot(here), :] = c_out[pl.ds(here, 1)][0]
     d_in[slot(here), :] = d_out[pl.ds(here, 1)][0]
     for t in others():
-        copy_to(c_out.at[t], c_in.at[slot(t)], c_s.at[t], c_r.at[t], device(t)).wait_recv()
-        copy_to(d_out.at[t], d_in.at[slot(t)], d_s.at[t], d_r.at[t], device(t)).wait_recv()
+        for k in range(HALVES):
+            give(c_out, c_in, c_s, c_r, t, k, t).wait_recv()
+            give(d_out, d_in, d_s, d_r, t, k, t).wait_recv()
+
+    def clean():
+        share(1, here, far).wait_send()
+        share(0, here, twin).wait_send()
+        share(2, far, twin).wait_send()
+        for t in others():
+            give_e(t).wait_send()
+            for k in range(HALVES):
+                give_c(t, k).wait_send()
+                give_d(t, k).wait_send()
+
+        @pl.when(side == 0)
+        def _():
+            for k in range(HALVES):
+                hop(0, k).wait_send()
+
+        @pl.when(side == 1)
+        def _():
+            for k in range(HALVES):
+                hop(1, k).wait_send()
 
     gram[...] = dot(c_in[...].T, d_in[...]).astype(BF16)
     own = width // streams
@@ -331,8 +383,12 @@
         )
 
         def product():
-            sl = pl.ds(base, own)
-            part[sl, :] = (dot(emb_t[sl, :], d_in[...]) + dot(basis[sl, :], gram[...])).astype(BF16)
+            @pl.loop(0, own // PR)
+            def _(i):
+                sl = rows_at(base + i * PR, PR)
+                value = dot(emb_t[sl, :], d_in[...]) + dot(basis[sl, :], gram[...])
+                part[sl, :] = value.astype(BF16)
+
             for k in range(4):
                 scat[k].start()
 
@@ -363,6 +419,8 @@
                 mid[st, sub(pos2), :], mid_in[st, 0], mid_in[st, 1], mid_in[st, 2]
             )
             swap.start()
+            for m in scat:
+                m.wait_send()
 
         def total_done():
             swap.wait_recv()
@@ -375,6 +433,8 @@
                 m.wait_recv()
             gath[0].start()
             gath[1].start()
+            for m in scat2 + [swap] + gath2:
+                m.wait_send()
 
         def forward_right():
             gath[0].wait_recv()
@@ -390,7 +450,7 @@
             store.start()
 
         def finish():
-            for m in scat + scat2 + [swap] + gath2 + gath:
+            for m in gath:
                 m.wait_send()
             store.wait()
 
@@ -404,26 +464,12 @@
     order = sorted(
         (times[0][k] + times[1][k] * (st // 2), st, k) for st in range(streams) for k in range(10)
     )
-    for _, st, k in order:
+    for n, (_, st, k) in enumerate(order):
+        if n == streams:
+            clean()
         made[st][0][k]()
     for st in range(streams):
         made[st][1]()
-
-    share(1, here, far).wait_send()
-    share(0, here, twin).wait_send()
-    share(2, far, twin).wait_send()
-    for t in others():
-        give_e(t).wait_send()
-        give_c(t).wait_send()
-        give_d(t).wait_send()
-
-    @pl.when(side == 0)
-    def _():
-        hop(0).wait_send()
-
-    @pl.when(side == 1)
-    def _():
-        hop(1).wait_send()
 
 
 def place(src, dst, hold, sem):
@@ -471,6 +517,7 @@
         pltpu.VMEM((rows, table.shape[0]), BF16),
         pltpu.VMEM((rank, hidden), BF16),
         pltpu.VMEM((group, 2, rank, hidden), BF16),
+        pltpu.VMEM((group, 2, hidden, rank), BF16),
         pltpu.VMEM((rows, hidden), BF16),
         pltpu.VMEM((group, mine, hidden), BF16),
         pltpu.VMEM((group, mine, hidden), F32),
@@ -481,6 +528,8 @@
         pltpu.VMEM((rows, rank), BF16),
         pltpu.VMEM((rows, hidden), BF16),
         pltpu.VMEM((rows, 1), F32),
+        pltpu.VMEM((mine, rank), F32),
+        pltpu.VMEM((mine, 1), F32),
         pltpu.VMEM((2, mine, rank), BF16),
         pltpu.VMEM((2, mine, rank), BF16),
         pltpu.VMEM((streams, 6, b1 // 2, hidden), BF16),
@@ -488,8 +537,8 @@
         pltpu.VMEM((streams, 3, b2, hidden), BF16),
         pltpu.VMEM((streams, b2, hidden), BF16),
         dma((4, tiles)), dma((3,)), dma((3,)),
-        dma((group,)), dma((group,)), dma((group,)), dma((group,)), dma((group,)), dma((group,)),
-        dma((2,)), dma((2,)), dma((streams * 17,)), dma((streams * 17,)), dma((streams,)),
+        dma((group,)), dma((group,)), dma((group, HALVES)), dma((group, HALVES)),
+        dma((group, HALVES)), dma((group, HALVES)), dma((2, HALVES)), dma((2, HALVES)), dma((streams * 17,)), dma((streams * 17,)), dma((streams,)),
     ]
     out = pl.pallas_call(
         functools.partial(kernel, streams, TIMES[streams]),

time: 82.6 us -> 81.7 us (0.989); the launches traced: 81.5 us -> 81.5 us
  no operation moved by 1% of the time
where the time goes in v4:
time: 81.7 us; the launch traced here: 81.5 us
  Pallas kernels  81.5 us (100%)
    pallas_call x1, Pallas kernels, on_device(): pl.pallas_call(functools.partial(kernel, streams, TIMES[streams]), out_sh...  79.1 us
    pallas_call x1, Pallas kernels, on_device(): pl.pallas_call(place, out_shape=jax.ShapeDtypeStruct((width, hidden), BF1...  2.42 us

profile of v4, /device:TPU:2, one launch (start us, length us, event | category | flops | bytes accessed | tf_op | source)
XLA Modules:
  0.0 81.5 jit_solution(16174982311862521304)
XLA Ops:
  0.0 79.1 %shard_map.73.src = bf16[4096,256]{1,0:T(8,128)(2,1)} custom-call(s32[2,8,256]{2,1,0:T(8,128)} %bitcast.8, s32[2,256]{1,0:T(2,128)} %len_ref.1, bf16[256,4096]{1,0:T(8,128)(2,1)} %table_hbm.1, bf16[4096,256]{1,0:T(8,128)(2,1)} %basis_hbm.1, bf16[4096,256]{1,0:T(8,128)(2,1)} %bitcast.5, bf16[4096,256]{1,0:T(8,128)(2,1)} %bitcast.6, bf16[512,256]{1,0:T(8,128)(2,1)} %bitcast.7), custom_call_target="tpu_custom_call" | custom-call | tf_op jit(solution)/shard_map/pallas_call | solution.py:543
  79.1 2.4 %shard_map.74 = bf16[4096,256]{1,0:T(8,128)(2,1)} custom-call(bf16[4096,256]{1,0:T(8,128)(2,1)} %shard_map.73.src), custom_call_target="tpu_custom_call" | custom-call | tf_op jit(solution)/shard_map/pallas_call | solution.py:553

commit v5 on v4

--- a/solution.py
+++ b/solution.py
@@ -30,7 +30,7 @@
     streams, times,
     ids_ref, len_ref, table_hbm, basis_hbm, down_hbm, up_hbm, dcoef_hbm, out_hbm,
     table, basis, down, up, emb, emb_t, part, res,
-    acc_s, acc_e, counts, gram, shared, turned, own_e, all_e,
+    acc_s, acc_e, counts, gram, shared, turned, chain, own_e, all_e,
     z_st, xb_st, r_st, c_out, d_out, c_in, d_in, small, fb_st, e2_st, hop_out, hop_in,
     big_in, mid, mid_in, z_in,
     load_sem, mu_s, mu_r, e_s, e_r, c_s, c_r, d_s, d_r, hop_s, hop_r, ar_s, ar_r, st_sem,
@@ -175,6 +175,8 @@
         def _(s):
             for n in range(2):
                 turned[s, n] = shared[s, n].T
+            for s in range(group - 1):
+                chain[s, 2] = dot(turned[s + 1, 0], turned[s, 1]).astype(BF16)
 
         @pl.loop(0, tiles)
         def _(i):
@@ -185,6 +187,9 @@
 
     share(0, twin, twin).wait_recv()
     share(2, far_twin, twin).wait_recv()
+    for s in range(group - 1):
+        chain[s, 0] = dot(shared[s, 1], shared[s + 1, 0]).astype(BF16)
+        chain[s, 1] = dot(shared[s, 1], gram[...]).astype(BF16)
     for t in others():
         copy_to(own_e.at[slot(t)], all_e.at[t], e_s.at[t], e_r.at[t], device(t)).wait_recv()
 
@@ -219,37 +224,45 @@
     def up_part(k, coef):
         fb, e2 = fb_st[cut(k), :], e2_st[cut(k), :]
 
-        def step_up(s, coef):
+        cg = cm = None
+        for s in range(group):
             cb = coef.astype(BF16)
             c_out[s, cut(k)] = cb
-            cg = dot(cb, gram[...])
+            if s == 0:
+                cg = dot(cb, gram[...])
+                cm = dot(cb, shared[0, 0])
             xb = fb + cg
             sq = e2 + jnp.sum(coef * (fb + xb), axis=1, keepdims=True)
             r = lax.rsqrt(jnp.maximum(sq, 0.0) * inv + 1e-06)
-            z = r * (all_e[s, cut(k)].astype(F32) + dot(cb, shared[s, 0]))
+            z = r * (all_e[s, cut(k)].astype(F32) + cm)
             z_st[s, cut(k)] = z
             xb_st[s, cut(k)] = xb
             r_st[s, cut(k)] = r
             act = (z * sigmoid(z)).astype(BF16)
-            return coef + dot(act, shared[s, 1])
-
-        return lax.fori_loop(0, group, step_up, coef, unroll=True)
+            if s < group - 1:
+                cm = dot(cb, shared[s + 1, 0]) + dot(act, chain[s, 0])
+                cg = cg + dot(act, chain[s, 1])
+            coef = coef + dot(act, shared[s, 1])
+        return coef
 
     def down_part(k, grad, then):
-        def step_down(i, grad):
-            s = group - 1 - i
-            da = dot(grad.astype(BF16), turned[s, 1])
+        da = dot(grad.astype(BF16), turned[group - 1, 1])
+        for s in reversed(range(group)):
             z = z_st[s, cut(k)]
             r = r_st[s, cut(k)]
             sig = sigmoid(z)
-            dz = da * sig * (1.0 + z * (1.0 - sig))
+            dz = da * (sig * (1.0 + z * (1.0 - sig)))
             d_out[s, cut(k)] = (r * dz).astype(BF16)
             then(s)
+            dzb = dz.astype(BF16)
             mean = jnp.sum(dz * z, axis=1, keepdims=True) * inv
-            back = dot(dz.astype(BF16), turned[s, 0])
-            return grad + r * (back - (r * mean) * xb_st[s, cut(k)])
-
-        return lax.fori_loop(0, group, step_down, grad, unroll=True)
+            if s > 0:
+                da = dot(grad.astype(BF16), turned[s - 1, 1]) + r * (
+                    dot(dzb, chain[s - 1, 2])
+                    - (r * mean) * dot(xb_st[s, cut(k)].astype(BF16), turned[s - 1, 1])
+                )
+            grad = grad + r * (dot(dzb, turned[s, 0]) - (r * mean) * xb_st[s, cut(k)])
+        return grad
 
     @pl.when(side == 0)
     def _():
@@ -518,6 +531,7 @@
         pltpu.VMEM((rank, hidden), BF16),
         pltpu.VMEM((group, 2, rank, hidden), BF16),
         pltpu.VMEM((group, 2, hidden, rank), BF16),
+        pltpu.VMEM((group - 1, 3, hidden, hidden), BF16),
         pltpu.VMEM((rows, hidden), BF16),
         pltpu.VMEM((group, mine, hidden), BF16),
         pltpu.VMEM((group, mine, hidden), F32),

time: 81.7 us -> 80.5 us (0.985)
  Pallas kernels: 81.5 us -> 80.3 us
    pallas_call x1, Pallas kernels: 79.1 us -> 77.9 us  [on_device(): pl.pallas_call(functools.partial(kernel, streams, TIMES[streams]), out_sh...]
where the time goes in v5:
time: 80.5 us; the launch traced here: 80.3 us
  Pallas kernels  80.3 us (100%)
    pallas_call x1, Pallas kernels, on_device(): pl.pallas_call(functools.partial(kernel, streams, TIMES[streams]), out_sh...  77.9 us
    pallas_call x1, Pallas kernels, on_device(): pl.pallas_call(place, out_shape=jax.ShapeDtypeStruct((width, hidden), BF1...  2.42 us

profile of v5, /device:TPU:2, one launch (start us, length us, event | category | flops | bytes accessed | tf_op | source)
XLA Modules:
  0.0 80.3 jit_solution(17694910752694093867)
XLA Ops:
  0.0 77.9 %shard_map.73.src = bf16[4096,256]{1,0:T(8,128)(2,1)} custom-call(s32[2,8,256]{2,1,0:T(8,128)} %bitcast.8, s32[2,256]{1,0:T(2,128)} %len_ref.1, bf16[256,4096]{1,0:T(8,128)(2,1)} %table_hbm.1, bf16[4096,256]{1,0:T(8,128)(2,1)} %basis_hbm.1, bf16[4096,256]{1,0:T(8,128)(2,1)} %bitcast.5, bf16[4096,256]{1,0:T(8,128)(2,1)} %bitcast.6, bf16[512,256]{1,0:T(8,128)(2,1)} %bitcast.7), custom_call_target="tpu_custom_call" | custom-call | tf_op jit(solution)/shard_map/pallas_call | solution.py:557
  77.9 2.4 %shard_map.74 = bf16[4096,256]{1,0:T(8,128)(2,1)} custom-call(bf16[4096,256]{1,0:T(8,128)(2,1)} %shard_map.73.src), custom_call_target="tpu_custom_call" | custom-call | tf_op jit(solution)/shard_map/pallas_call | solution.py:567

commit v6 on v5

--- a/solution.py
+++ b/solution.py
@@ -10,12 +10,18 @@
 MESH = pl.DeviceIdType.MESH
 RING = 4
 F32, BF16 = jnp.float32, jnp.bfloat16
-STREAMS = 4
 HALVES = 1
 PR = 256
-TIMES = {
-    4: ((0, 4.2, 4.2, 8.4, 13, 18.5, 23, 28, 28, 32), (1, 2.8, 2.8, 2.8, 2.8, 2.8, 2.8, 2.8, 2.8, 2.8)),
-}
+SIZES = (512,) * 8
+ORDER = (
+    (0, 0), (1, 0), (2, 0), (3, 0), (4, 0), (5, 0), (6, 0), (7, 0), (0, 1), (0, 2), (1, 1), (1, 2),
+    (2, 1), (2, 2), (3, 1), (3, 2), (4, 1), (4, 2), (5, 1), (5, 2), (6, 1), (6, 2), (7, 1), (7, 2),
+    (0, 3), (1, 3), (2, 3), (3, 3), (4, 3), (5, 3), (6, 3), (7, 3), (0, 4), (1, 4), (2, 4), (3, 4),
+    (4, 4), (5, 4), (6, 4), (7, 4), (0, 5), (1, 5), (2, 5), (3, 5), (4, 5), (5, 5), (6, 5), (7, 5),
+    (0, 6), (1, 6), (2, 6), (3, 6), (4, 6), (5, 6), (6, 6), (7, 6), (0, 7), (0, 8), (1, 7), (1, 8),
+    (2, 7), (2, 8), (3, 7), (3, 8), (4, 7), (4, 8), (5, 7), (5, 8), (6, 7), (6, 8), (7, 7), (7, 8),
+    (0, 9), (1, 9), (2, 9), (3, 9), (4, 9), (5, 9), (6, 9), (7, 9),
+)
 
 
 def dot(a, b, dims=((1,), (0,))):
@@ -27,12 +33,12 @@
 
 
 def kernel(
-    streams, times,
+    sizes, order,
     ids_ref, len_ref, table_hbm, basis_hbm, down_hbm, up_hbm, dcoef_hbm, out_hbm,
     table, basis, down, up, emb, emb_t, part, res,
     acc_s, acc_e, counts, gram, shared, turned, chain, own_e, all_e,
     z_st, xb_st, r_st, c_out, d_out, c_in, d_in, small, fb_st, e2_st, hop_out, hop_in,
-    big_in, mid, mid_in, z_in,
+    big_in, mids, mid_in, z_in,
     load_sem, mu_s, mu_r, e_s, e_r, c_s, c_r, d_s, d_r, hop_s, hop_r, ar_s, ar_r, st_sem,
 ):
     sections = lax.axis_size("section")
@@ -170,14 +176,14 @@
     share(1, far, far).wait_recv()
     share(2, far, twin).start()
 
-    def flip():
-        @pl.loop(0, group)
-        def _(s):
+    def turn_weights():
+        for s in range(group):
             for n in range(2):
                 turned[s, n] = shared[s, n].T
-            for s in range(group - 1):
-                chain[s, 2] = dot(turned[s + 1, 0], turned[s, 1]).astype(BF16)
-
+        for s in range(group - 1):
+            chain[s, 2] = dot(turned[s + 1, 0], turned[s, 1]).astype(BF16)
+
+    def flip():
         @pl.loop(0, tiles)
         def _(i):
             sl = pl.ds(pl.multiple_of(i * tile, tile), tile)
@@ -273,6 +279,7 @@
         for t in others():
             for k in range(HALVES):
                 give_c(t, k).start()
+        turn_weights()
         flip()
         for k in range(HALVES):
             hop(1, k).wait_recv()
@@ -288,7 +295,7 @@
     def _():
         last = pltpu.make_async_copy(dcoef_hbm.at[slot(here)], hop_in.at[1], st_sem.at[0])
         last.start()
-        flip()
+        turn_weights()
         last.wait()
         for k in range(HALVES):
             hop(0, k).wait_recv()
@@ -300,6 +307,7 @@
             for k in range(HALVES):
                 give_c(t, k).start()
                 give_d(t, k).start()
+        flip()
 
     c_in[slot(here), :] = c_out[pl.ds(here, 1)][0]
     d_in[slot(here), :] = d_out[pl.ds(here, 1)][0]
@@ -329,9 +337,6 @@
                 hop(1, k).wait_send()
 
     gram[...] = dot(c_in[...].T, d_in[...]).astype(BF16)
-    own = width // streams
-    b1, b2 = own // RING, own // RING // RING
-    hf = b1 // 2
     per = 17
 
     def rows_at(start, size):
@@ -349,7 +354,14 @@
         return total_.astype(BF16)
 
     def stream(st):
-        base = st * own
+        own = sizes[st]
+        base = sum(sizes[:st])
+        b1, b2 = own // RING, own // RING // RING
+        hf = b1 // 2
+        big = big_in.at[pl.ds(base * 3 // 4, own * 3 // 4)]
+        mid = mids.at[pl.ds(base * 5 // 16, own * 5 // 16)]
+        subs = mid_in.at[pl.ds(base * 3 // 16, own * 3 // 16)]
+        zin = z_in.at[pl.ds(base // 16, b2)]
         pos, pos2 = (cx, cy) if st % 2 == 0 else (cy, cx)
         right, left, opposite = turn(pos, 1), turn(pos, 3), turn(pos, 2)
         n0 = st * per
@@ -361,7 +373,7 @@
             return rows_at(base + owner * b1 + part_no * hf, hf)
 
         def over(k, owner, part_no, to):
-            return send(k, part.at[blk(owner, part_no)], big_in.at[st, k], along(st, 0, to))
+            return send(k, part.at[blk(owner, part_no)], big.at[pl.ds(k * hf, hf)], along(st, 0, to))
 
         scat = [
             over(0, opposite, 0, right), over(1, opposite, 1, left), over(2, right, 1, right),
@@ -372,11 +384,11 @@
             return rows_at(v * b2, b2)
 
         scat2 = [
-            send(5 + o, mid.at[st, sub(turn(pos2, o))], mid_in.at[st, o - 1],
+            send(5 + o, mid.at[sub(turn(pos2, o))], subs.at[pl.ds((o - 1) * b2, b2)],
                  along(st, 1, turn(pos2, o)))
             for o in range(1, RING)
         ]
-        swap = send(9, mid.at[st, pl.ds(b1, b2)], z_in.at[st], at(cx, cy, 1 - zh))
+        swap = send(9, mid.at[pl.ds(b1, b2)], zin, at(cx, cy, 1 - zh))
         mine_sl = rows_at(base + pos * b1 + pos2 * b2, b2)
         gath2 = [
             send(9 + o, res.at[mine_sl], res.at[mine_sl], along(st, 1, turn(pos2, o)))
@@ -407,29 +419,29 @@
 
         def pass_right():
             scat[0].wait_recv()
-            part[blk(right, 0), :] = add(part[blk(right, 0), :], big_in[st, 0])
+            part[blk(right, 0), :] = add(part[blk(right, 0), :], big[0 * hf : 1 * hf, :])
             scat[4].start()
 
         def pass_left():
             scat[1].wait_recv()
-            part[blk(left, 1), :] = add(part[blk(left, 1), :], big_in[st, 1])
+            part[blk(left, 1), :] = add(part[blk(left, 1), :], big[1 * hf : 2 * hf, :])
             scat[5].start()
 
         def block_done():
             scat[3].wait_recv()
             scat[4].wait_recv()
-            mid[st, 0:hf, :] = add(part[blk(pos, 0), :], big_in[st, 3], big_in[st, 4])
+            mid[0:hf, :] = add(part[blk(pos, 0), :], big[3 * hf : 4 * hf, :], big[4 * hf : 5 * hf, :])
             scat[2].wait_recv()
             scat[5].wait_recv()
-            mid[st, hf:b1, :] = add(part[blk(pos, 1), :], big_in[st, 2], big_in[st, 5])
+            mid[hf:b1, :] = add(part[blk(pos, 1), :], big[2 * hf : 3 * hf, :], big[5 * hf : 6 * hf, :])
             for m in scat2:
                 m.start()
 
         def sub_done():
             for m in scat2:
                 m.wait_recv()
-            mid[st, b1 : b1 + b2, :] = add(
-                mid[st, sub(pos2), :], mid_in[st, 0], mid_in[st, 1], mid_in[st, 2]
+            mid[b1 : b1 + b2, :] = add(
+                mid[sub(pos2), :], subs[0 * b2 : 1 * b2, :], subs[1 * b2 : 2 * b2, :], subs[2 * b2 : 3 * b2, :]
             )
             swap.start()
             for m in scat:
@@ -437,7 +449,7 @@
 
         def total_done():
             swap.wait_recv()
-            res[mine_sl, :] = add(mid[st, b1 : b1 + b2, :], z_in[st])
+            res[mine_sl, :] = add(mid[b1 : b1 + b2, :], zin[...])
             for m in gath2:
                 m.start()
 
@@ -473,11 +485,9 @@
         ]
         return stages, finish
 
+    streams = len(sizes)
     made = [stream(st) for st in range(streams)]
-    order = sorted(
-        (times[0][k] + times[1][k] * (st // 2), st, k) for st in range(streams) for k in range(10)
-    )
-    for n, (_, st, k) in enumerate(order):
+    for n, (st, k) in enumerate(order):
         if n == streams:
             clean()
         made[st][0][k]()
@@ -509,10 +519,9 @@
     group = sections // 2
     mine = rows // group
     tiles = 8
-    streams = STREAMS
+    sizes = SIZES
+    streams = len(sizes)
     ids = jnp.transpose(byte_ids, (0, 2, 1))
-    b1 = width // streams // RING
-    b2 = b1 // RING
     vmem = pl.BlockSpec(memory_space=pltpu.VMEM)
     hbm = pl.BlockSpec(memory_space=pl.ANY)
     dma = pltpu.SemaphoreType.DMA
@@ -546,16 +555,16 @@
         pltpu.VMEM((mine, 1), F32),
         pltpu.VMEM((2, mine, rank), BF16),
         pltpu.VMEM((2, mine, rank), BF16),
-        pltpu.VMEM((streams, 6, b1 // 2, hidden), BF16),
-        pltpu.VMEM((streams, b1 + b2, hidden), BF16),
-        pltpu.VMEM((streams, 3, b2, hidden), BF16),
-        pltpu.VMEM((streams, b2, hidden), BF16),
+        pltpu.VMEM((width * 3 // 4, hidden), BF16),
+        pltpu.VMEM((width * 5 // 16, hidden), BF16),
+        pltpu.VMEM((width * 3 // 16, hidden), BF16),
+        pltpu.VMEM((width // 16, hidden), BF16),
         dma((4, tiles)), dma((3,)), dma((3,)),
         dma((group,)), dma((group,)), dma((group, HALVES)), dma((group, HALVES)),
         dma((group, HALVES)), dma((group, HALVES)), dma((2, HALVES)), dma((2, HALVES)), dma((streams * 17,)), dma((streams * 17,)), dma((streams,)),
     ]
     out = pl.pallas_call(
-        functools.partial(kernel, streams, TIMES[streams]),
+        functools.partial(kernel, sizes, ORDER),
         out_shape=jax.ShapeDtypeStruct((width, hidden), BF16),
         in_specs=[vmem, vmem, hbm, hbm, hbm, hbm, hbm],
         out_specs=hbm,

time: 80.5 us -> 78.5 us (0.975)
  Pallas kernels: 80.3 us -> 78.3 us
    pallas_call x1, Pallas kernels: 77.9 us -> 75.9 us  [on_device(): pl.pallas_call(functools.partial(kernel, sizes, ORDER), out_shape=jax.Sha...]
where the time goes in v6:
time: 78.5 us; the launch traced here: 78.3 us
  Pallas kernels  78.3 us (100%)
    pallas_call x1, Pallas kernels, on_device(): pl.pallas_call(functools.partial(kernel, sizes, ORDER), out_shape=jax.Sha...  75.9 us
    pallas_call x1, Pallas kernels, on_device(): pl.pallas_call(place, out_shape=jax.ShapeDtypeStruct((width, hidden), BF1...  2.42 us

profile of v6, /device:TPU:2, one launch (start us, length us, event | category | flops | bytes accessed | tf_op | source)
XLA Modules:
  0.0 78.3 jit_solution(1711570118194004933)
XLA Ops:
  0.0 75.9 %shard_map.73.src = bf16[4096,256]{1,0:T(8,128)(2,1)} custom-call(s32[2,8,256]{2,1,0:T(8,128)} %bitcast.8, s32[2,256]{1,0:T(2,128)} %len_ref.1, bf16[256,4096]{1,0:T(8,128)(2,1)} %table_hbm.1, bf16[4096,256]{1,0:T(8,128)(2,1)} %basis_hbm.1, bf16[4096,256]{1,0:T(8,128)(2,1)} %bitcast.5, bf16[4096,256]{1,0:T(8,128)(2,1)} %bitcast.6, bf16[512,256]{1,0:T(8,128)(2,1)} %bitcast.7), custom_call_target="tpu_custom_call" | custom-call | tf_op jit(solution)/shard_map/pallas_call | solution.py:566
  75.9 2.4 %shard_map.74 = bf16[4096,256]{1,0:T(8,128)(2,1)} custom-call(bf16[4096,256]{1,0:T(8,128)(2,1)} %shard_map.73.src), custom_call_target="tpu_custom_call" | custom-call | tf_op jit(solution)/shard_map/pallas_call | solution.py:576

commit v7 on v6

--- a/solution.py
+++ b/solution.py
@@ -11,7 +11,7 @@
 RING = 4
 F32, BF16 = jnp.float32, jnp.bfloat16
 HALVES = 1
-PR = 256
+PR = 512
 SIZES = (512,) * 8
 ORDER = (
     (0, 0), (1, 0), (2, 0), (3, 0), (4, 0), (5, 0), (6, 0), (7, 0), (0, 1), (0, 2), (1, 1), (1, 2),

time: 78.5 us -> 78.4 us (level)
  no operation moved by 1% of the time
where the time goes in v7:
time: 78.4 us; the launch traced here: 78.2 us
  Pallas kernels  78.2 us (100%)
    pallas_call x1, Pallas kernels, on_device(): pl.pallas_call(functools.partial(kernel, sizes, ORDER), out_shape=jax.Sha...  75.8 us
    pallas_call x1, Pallas kernels, on_device(): pl.pallas_call(place, out_shape=jax.ShapeDtypeStruct((width, hidden), BF1...  2.42 us

profile of v7, /device:TPU:2, one launch (start us, length us, event | category | flops | bytes accessed | tf_op | source)
XLA Modules:
  0.0 78.2 jit_solution(10131820434112072233)
XLA Ops:
  0.0 75.8 %shard_map.73.src = bf16[4096,256]{1,0:T(8,128)(2,1)} custom-call(s32[2,8,256]{2,1,0:T(8,128)} %bitcast.8, s32[2,256]{1,0:T(2,128)} %len_ref.1, bf16[256,4096]{1,0:T(8,128)(2,1)} %table_hbm.1, bf16[4096,256]{1,0:T(8,128)(2,1)} %basis_hbm.1, bf16[4096,256]{1,0:T(8,128)(2,1)} %bitcast.5, bf16[4096,256]{1,0:T(8,128)(2,1)} %bitcast.6, bf16[512,256]{1,0:T(8,128)(2,1)} %bitcast.7), custom_call_target="tpu_custom_call" | custom-call | tf_op jit(solution)/shard_map/pallas_call | solution.py:566
  75.8 2.4 %shard_map.74 = bf16[4096,256]{1,0:T(8,128)(2,1)} custom-call(bf16[4096,256]{1,0:T(8,128)(2,1)} %shard_map.73.src), custom_call_target="tpu_custom_call" | custom-call | tf_op jit(solution)/shard_map/pallas_call | solution.py:576
